TPU v7x, 512 devices: a whole 4x4x16 slice. The times are simulated.
512 devices in a mesh: seq: 64 (over z, x_lo, core), head: 8 (over x_hi, y).
Axes of the slice: x: 4 (x_hi: 2, x_lo: 2; x = x_hi * 2 + x_lo), y: 4, z: 16, core: 2. Of those that a mesh axis runs over, the one named last changes fastest.
Arguments:
- queries: bfloat16 [16384, 8192], P('seq', 'head'), may hold values from -200 to 200
- layer_key_rows: bfloat16 [16384, 1024], P('seq', 'head'), may hold values from -7 to 7
- layer_value_rows: bfloat16 [16384, 1024], P('seq', 'head'), may hold values from -6 to 6
- output_gradient: bfloat16 [16384, 8192], P('seq', 'head'), may hold values from -24 to 24
- output_row_sums: float32 [64, 16384], P('head', 'seq'), may hold values from -72 to 72
- shifted_head_flags: int32 [64], P('head'), may hold values from 0 to 1, as said below
- inputs: bfloat16 [16384, 8192], P('seq', 'head'), may hold values from -6 to 6
- adapter_down_weight: bfloat16 [3, 16, 8192], P(None, None, 'head'), may hold values from -0.0625 to 0.0625
- query_up_weight: bfloat16 [16, 8192], P(None, 'head'), may hold values from -0.75 to 0.75
- key_value_up_weight: bfloat16 [2, 16, 1024], P(None, None, 'head'), may hold values from -0.75 to 0.75
Outputs:
- grad_inputs: bfloat16 [16384, 8192], P('seq', 'head')
- key_value_gradient: bfloat16 [2, 16384, 1024], P(None, 'seq', 'head')
- down_gradient: float32 [3, 16, 8192], P(None, None, 'head')
- grad_up_q: float32 [16, 8192], P(None, 'head')
- grad_up_kv: float32 [2, 16, 1024], P(None, None, 'head')
Inputs may be any that keep to these rules, and one draw needn't show every extreme that they name: `shifted_head_flags`: exactly half of the 64 heads have 1.
All inputs are finite; a program needn't handle non-finite values.
Results may differ from a plain program's by a relative error of at most 0.013.
Values may be sent and summed in bfloat16 or wider, within the bound.
A program may use at most 64 MiB of HBM per device.

v0:
```python
import math

import jax
import jax.numpy as jnp
from jax import lax
from jax.sharding import PartitionSpec as P

HEAD_SIZE = 128
GROUP = 1024
SHIFT = 512


adapter_scale = 2.0
masked_score = -1e30


def shifted(shard, axis, by):
    devices = lax.axis_size(axis)
    return lax.ppermute(shard, axis, [(i, (i + by) % devices) for i in range(devices)])


def visible_pairs(query_pos, key_pos, shift_flags, whole_len):
    offsets = shift_flags[:, None] * SHIFT
    query_place = (query_pos[None, :] - offsets) % whole_len
    key_place = (key_pos[None, :] - offsets) % whole_len
    same_group = query_place[:, :, None] // GROUP == key_place[:, None, :] // GROUP
    return same_group & (key_place[:, None, :] <= query_place[:, :, None])


def block_backward(
    query_block, key_window, value_window, grad_block, term_block, visible, score_scale
):
    scores = (
        jnp.einsum("thd,kd->htk", query_block, key_window, preferred_element_type=jnp.float32)
        * score_scale
    )
    scores = jnp.where(visible, scores, masked_score)
    row_max = jnp.max(scores, axis=2, keepdims=True)
    weights = jnp.where(visible, jnp.exp(scores - row_max), 0.0)
    prob_rows = weights / jnp.sum(weights, axis=2, keepdims=True)
    prob_low = prob_rows.astype(jnp.bfloat16)
    grad_values = jnp.einsum(
        "htk,thd->kd", prob_low, grad_block, preferred_element_type=jnp.float32
    )
    grad_probs = jnp.einsum(
        "thd,kd->htk", grad_block, value_window, preferred_element_type=jnp.float32
    )
    grad_scores = (prob_rows * (grad_probs - term_block[:, :, None])).astype(jnp.bfloat16)
    grad_query = (
        jnp.einsum("htk,kd->thd", grad_scores, key_window, preferred_element_type=jnp.float32)
        * score_scale
    ).astype(jnp.bfloat16)
    grad_keys = (
        jnp.einsum("htk,thd->kd", grad_scores, query_block, preferred_element_type=jnp.float32)
        * score_scale
    )
    return (grad_query, grad_keys, grad_values)


def contract_rows(left_side, right_side):
    return lax.dot_general(
        left_side, right_side, (((0,), (0,)), ((), ())), preferred_element_type=jnp.float32
    )


def contracted_columns(left_side, right_side):
    return lax.dot_general(
        left_side, right_side, (((1,), (1,)), ((), ())), preferred_element_type=jnp.float32
    )


def per_device(
    queries,
    layer_key_rows,
    layer_value_rows,
    output_gradient,
    output_row_sums,
    shifted_head_flags,
    inputs,
    adapter_down_weight,
    query_up_weight,
    key_value_up_weight,
):
    seq_count = lax.axis_size("seq")
    seq_index = lax.axis_index("seq")
    tokens_here = queries.shape[0]
    whole_len = tokens_here * seq_count
    reach_count = max(1, GROUP // tokens_here - 1)
    kv_local = layer_key_rows.shape[1] // HEAD_SIZE
    heads_here = queries.shape[1] // HEAD_SIZE
    per_kv = heads_here // kv_local
    block_heads = math.gcd(per_kv, max(1, 512 // tokens_here))
    score_scale = HEAD_SIZE ** (-0.5)
    adapter_rank_width = adapter_down_weight.shape[1]
    flattened_down = adapter_down_weight.reshape(
        3 * adapter_rank_width, adapter_down_weight.shape[2]
    )
    down_part = contracted_columns(inputs, flattened_down)
    down_in = lax.psum(down_part, "head")
    kv_own = jnp.stack([layer_key_rows, layer_value_rows])
    earlier = []
    moving = kv_own
    for hop_index in range(reach_count):
        moving = shifted(moving, "seq", 1)
        earlier.append(moving)
    positions = jnp.arange(tokens_here, dtype=jnp.int32)
    own_pos = seq_index * tokens_here + positions
    key_pos = jnp.concatenate(
        [
            (seq_index - hop_index) % seq_count * tokens_here + positions
            for hop_index in range(reach_count, 0, -1)
        ]
        + [own_pos]
    )
    window = jnp.concatenate(
        [earlier[hop_index - 1] for hop_index in range(reach_count, 0, -1)] + [kv_own], axis=1
    )
    query_heads = queries.reshape(tokens_here, heads_here, HEAD_SIZE)
    grad_heads = output_gradient.reshape(tokens_here, heads_here, HEAD_SIZE)
    query_grads = []
    key_window = window[0]
    value_window = window[1]
    key_acc = jnp.zeros(key_window.shape, jnp.float32)
    value_acc = jnp.zeros(value_window.shape, jnp.float32)
    for head_start in range(0, per_kv, block_heads):
        head_stop = head_start + block_heads
        visible = visible_pairs(
            own_pos, key_pos, shifted_head_flags[head_start:head_stop], whole_len
        )
        grad_query, grad_keys, grad_values = block_backward(
            query_heads[:, head_start:head_stop],
            key_window,
            value_window,
            grad_heads[:, head_start:head_stop],
            output_row_sums[head_start:head_stop],
            visible,
            score_scale,
        )
        query_grads.append(grad_query)
        key_acc = key_acc + grad_keys
        value_acc = value_acc + grad_values
    query_gradient_rows = jnp.concatenate(query_grads, axis=1).reshape(
        tokens_here, heads_here * HEAD_SIZE
    )
    window_grads = jnp.stack([key_acc, value_acc])
    pieces = [
        window_grads[
            :, (reach_count - hop_index) * tokens_here : (reach_count - hop_index + 1) * tokens_here
        ]
        for hop_index in range(reach_count + 1)
    ]
    carried = pieces[reach_count]
    for hop_index in range(reach_count, 0, -1):
        carried = shifted(carried, "seq", -1) + pieces[hop_index - 1]
    key_value_gradient = carried.astype(jnp.bfloat16)
    up_part = jnp.concatenate(
        [
            contracted_columns(query_gradient_rows, query_up_weight),
            contracted_columns(key_value_gradient[0], key_value_up_weight[0]),
            contracted_columns(key_value_gradient[1], key_value_up_weight[1]),
        ],
        axis=1,
    )
    up_backward_term = lax.psum(up_part, "head")
    down_low = down_in.astype(jnp.bfloat16)
    up_low = up_backward_term.astype(jnp.bfloat16)
    grad_inputs = (
        adapter_scale * jnp.dot(up_low, flattened_down, preferred_element_type=jnp.float32)
    ).astype(jnp.bfloat16)
    down_term = contract_rows(up_low, inputs)
    up_q_term = contract_rows(down_low[:, :adapter_rank_width], query_gradient_rows)
    up_kv_term = jnp.stack(
        [
            contract_rows(
                down_low[:, adapter_rank_width : 2 * adapter_rank_width], key_value_gradient[0]
            ),
            contract_rows(down_low[:, 2 * adapter_rank_width :], key_value_gradient[1]),
        ]
    )
    down_total_sum, up_q_sum, up_kv_sum = lax.psum((down_term, up_q_term, up_kv_term), "seq")
    multiplier = adapter_scale / math.sqrt(whole_len)
    down_gradient = multiplier * down_total_sum.reshape(
        3, adapter_rank_width, adapter_down_weight.shape[2]
    )
    return (
        grad_inputs,
        key_value_gradient,
        down_gradient,
        multiplier * up_q_sum,
        multiplier * up_kv_sum,
    )


def solution(mesh):
    placed = (
        P("seq", "head"),
        P("seq", "head"),
        P("seq", "head"),
        P("seq", "head"),
        P("head", "seq"),
        P("head"),
        P("seq", "head"),
        P(None, None, "head"),
        P(None, "head"),
        P(None, None, "head"),
    )
    return jax.shard_map(
        per_device,
        mesh=mesh,
        in_specs=placed,
        out_specs=(
            P("seq", "head"),
            P(None, "seq", "head"),
            P(None, None, "head"),
            P(None, "head"),
            P(None, None, "head"),
        ),
        check_vma=False,
    )
```

profile of v0, /device:TPU:1, one launch (start us, length us, event | category | flops | bytes accessed | tf_op | source)
XLA Modules:
  0.0 761.8 jit_solution(6059187465821301231)
XLA Ops:
  7.2 0.0 copy-start
  7.2 0.0 all-reduce.4.cloned.1.call-start
  7.3 1.0 pad_maximum_fusion.2
  8.2 4.5 collective-permute-start
  12.8 0.9 slice_multiply_fusion.3
  13.7 1.2 copy.23
  14.9 1.4 copy.25
  16.4 0.3 fusion.155
  16.7 0.2 and_select_fusion.6
  16.9 0.9 collective-permute-done
  17.9 1.9 collective-permute-start.1
  19.8 0.1 and_select_fusion.14
  19.9 7.0 collective-permute-done.1
  26.9 1.9 collective-permute-start.2
  28.8 6.4 collective-permute-done.2
  35.3 2.4 fusion.146
  37.7 3.0 convolution_bitcast_fusion.1
  40.7 0.4 fusion.7
  41.1 1.2 convolution_bitcast_fusion.5
  42.4 2.4 fusion.149
  44.8 3.0 convolution_bitcast_fusion.2
  47.8 1.3 fusion.9
  49.1 2.1 convolution_bitcast_fusion.6
  51.2 3.2 fusion.143
  54.5 3.0 convolution_bitcast_fusion
  57.5 1.3 fusion.5
  58.8 1.0 copy-done.1
  59.8 2.1 convolution_bitcast_fusion.4
  61.9 3.2 fusion.152
  65.2 2.2 fusion.11
  67.4 0.0 copy-done.15
  67.4 0.1 copy-done.19
  67.5 0.2 copy-done.20
  67.7 0.2 copy-done.21
  67.8 1.5 fusion.25
  69.3 1.3 fusion.21
  70.7 7.6 collective-permute-start.3
  78.3 0.3 fusion.33
  78.6 0.3 fusion.31
  79.0 0.5 collective-permute-done.3
  79.5 4.6 collective-permute-start.4
  84.1 0.3 fusion.32
  84.5 0.3 fusion.30
  84.8 0.0 copy-start.14
  84.8 2.3 collective-permute-done.4
  87.2 6.8 collective-permute-start.5
  94.0 0.1 pad_maximum_fusion
  94.1 0.2 fusion.156
  94.2 0.9 collective-permute-done.5
  95.2 0.0 copy-start.7
  95.2 0.1 fusion.114
  95.3 0.1 fusion.113
  95.4 35.7 %all-reduce.1 = (bf16[256,48]{0,1:T(8,128)(2,1)S(1)}, bf16[256,48]{0,1:T(8,128)(2,1)S(1)}) all-reduce(f32[256,48]{0,1:T(8,128)S(1)} %pad_maximum_fusion.3, f32[256,48]{0,1:T(8,128)S(1)} %fusion.155), channel_id=1, replica_groups=mesh['seq'=64,'head'=8] {'head'}, use_global_device_ids=true, to_apply=%region_8.9 | all-reduce | flops 24576 | bytes 147456 | tf_op jit(solution)/shard_map/psum | solution.py:164
  131.2 0.9 fusion.124
  132.0 0.1 convolution_bitcast_fusion.9
  132.2 0.1 convolution_bitcast_fusion.8
  132.3 216.7 %psum.39 = f32[2,16,128]{2,1,0:T(8,128)S(1)} all-reduce(f32[2,16,128]{2,1,0:T(8,128)S(1)} %pad_maximum_fusion.4), channel_id=1, replica_groups=mesh['seq'=64,'head'=8] {'seq'}, use_global_device_ids=true, to_apply=%region_12.13 | all-reduce | flops 4096 | bytes 32768 | tf_op jit(solution)/shard_map/psum | solution.py:180
  349.0 0.9 fusion.157
  349.9 0.0 all-reduce.4.cloned.1.call-update
  349.9 0.6 broadcast_multiply_fusion.2
  350.5 1.1 fusion.16
  351.6 400.3 %all-reduce.4.cloned.1.call-done = (f32[48,1024]{1,0:T(8,128)}, f32[16,1024]{1,0:T(8,128)}) async-done(((f32[48,1024]{1,0:T(8,128)}, f32[16,1024]{1,0:T(8,128)}), (f32[48,1024]{1,0:T(8,128)}, f32[16,1024]{1,0:T(8,128)})) %all-reduce.4.cloned.1.call-update) | async-done | bytes 262160 | tf_op jit(solution)/shard_map/psum | solution.py:180
  751.9 1.6 broadcast_multiply_fusion
  753.5 1.5 broadcast_multiply_fusion.1
  (47 shorter events, 0.3 us)
Async XLA Ops:
  7.2 9.3 %copy-start = (bf16[256,1024]{1,0:T(8,128)(2,1)S(1)}, bf16[256,1024]{1,0:T(8,128)(2,1)}, u32[]{:S(2)}) copy-start(bf16[256,1024]{1,0:T(8,128)(2,1)} %param.16) | copy-start | bytes 1572868
  7.2 28.1 %copy-start.10 = (bf16[256,128]{1,0:T(8,128)(2,1)S(1)}, bf16[256,128]{1,0:T(8,128)(2,1)}, u32[]{:S(2)}) copy-start(bf16[256,128]{1,0:T(8,128)(2,1)} %param.12) | copy-start | bytes 196612
  7.2 28.1 %copy-start.11 = (bf16[256,128]{1,0:T(8,128)(2,1)S(1)}, bf16[256,128]{1,0:T(8,128)(2,1)}, u32[]{:S(2)}) copy-start(bf16[256,128]{1,0:T(8,128)(2,1)} %param.11) | copy-start | bytes 196612
  7.2 9.2 %copy-start.9 = (bf16[3,16,1024]{2,1,0:T(8,128)(2,1)S(1)}, bf16[3,16,1024]{2,1,0:T(8,128)(2,1)}, u32[]{:S(2)}) copy-start(bf16[3,16,1024]{2,1,0:T(8,128)(2,1)} %param.17) | copy-start | bytes 294916
  7.2 21.6 %copy-start.13 = (f32[8,256]{1,0:T(8,128)S(1)}, f32[8,256]{1,0:T(8,128)}, u32[]{:S(2)}) copy-start(f32[8,256]{1,0:T(8,128)} %param.14) | copy-start | bytes 24580
  7.2 744.7 %all-reduce.4.cloned.1.call-start = ((), (), s32[]{:S(2)}) async-start(), calls=%async_computation | async-start | bytes 524288 | tf_op jit(solution)/shard_map/psum | solution.py:180
  8.2 9.6 %collective-permute-start = (bf16[2,256,128]{2,1,0:T(8,128)(2,1)S(1)}, bf16[2,256,128]{2,1,0:T(8,128)(2,1)S(1)}, u32[]{:S(2)}, u32[]{:S(2)}) collective-permute-start(bf16[2,256,128]{2,1,0:T(8,128)(2,1)S(1)} %pad_maximum_fusion.2), channel_id=1, source_target_pairs={{0,8},{8,16},{16,24},{24,32},{32,40},{40,48},{48,56},{56,64},{64,7... | collective-permute-start | bytes 393224 | tf_op jit(solution)/shard_map/ppermute | solution.py:19
  14.9 27.4 %copy-start.6 = (bf16[256,1024]{0,1:T(8,128)(2,1)}, bf16[256,1024]{0,1:T(8,128)(2,1)S(1)}, u32[]{:S(2)}) copy-start(bf16[256,1024]{0,1:T(8,128)(2,1)S(1)} %copy.23) | copy-start | bytes 1572868
  16.4 28.4 %copy-start.8 = (bf16[256,1024]{0,1:T(8,128)(2,1)}, bf16[256,1024]{0,1:T(8,128)(2,1)S(1)}, u32[]{:S(2)}) copy-start(bf16[256,1024]{0,1:T(8,128)(2,1)S(1)} %copy.25) | copy-start | bytes 1572868
  17.9 9.0 %collective-permute-start.1 = (bf16[2,256,128]{2,1,0:T(8,128)(2,1)S(1)}, bf16[2,256,128]{2,1,0:T(8,128)(2,1)S(1)}, u32[]{:S(2)}, u32[]{:S(2)}) collective-permute-start(bf16[2,256,128]{2,1,0:T(8,128)(2,1)S(1)} %collective-permute-done), channel_id=1, source_target_pairs={{0,8},{8,16},{16,24},{24,32},{32,40},{40,48},{48,56},{56,64},{64,7... | collective-permute-start | bytes 393224 | tf_op jit(solution)/shard_map/ppermute | solution.py:19
  26.9 8.4 %collective-permute-start.2 = (bf16[2,256,128]{2,1,0:T(8,128)(2,1)S(1)}, bf16[2,256,128]{2,1,0:T(8,128)(2,1)S(1)}, u32[]{:S(2)}, u32[]{:S(2)}) collective-permute-start(bf16[2,256,128]{2,1,0:T(8,128)(2,1)S(1)} %collective-permute-done.1), channel_id=1, source_target_pairs={{0,8},{8,16},{16,24},{24,32},{32,40},{40,48},{48,56},{56,64},{64,7... | collective-permute-start | bytes 393224 | tf_op jit(solution)/shard_map/ppermute | solution.py:19
  37.7 3.0 copy-start.16
  44.8 3.0 copy-start.17
  54.5 3.0 copy-start.18
  58.8 1.0 copy-start.1
  65.2 2.3 copy-start.15
  65.2 2.4 copy-start.19
  65.2 2.5 copy-start.20
  65.2 2.7 copy-start.21
  67.8 1.5 copy-start.3
  67.8 1.5 copy-start.4
  67.8 1.5 copy-start.5
  70.7 8.7 %collective-permute-start.3 = (f32[2,256,128]{2,1,0:T(8,128)S(1)}, f32[2,256,128]{2,1,0:T(8,128)S(1)}, u32[]{:S(2)}, u32[]{:S(2)}) collective-permute-start(f32[2,256,128]{2,1,0:T(8,128)S(1)} %fusion.72), channel_id=1, source_target_pairs={{0,504},{8,0},{16,8},{24,16},{32,24},{40,32},{48,40},{56,48},{64,5... | collective-permute-start | bytes 786440 | tf_op jit(solution)/shard_map/ppermute | solution.py:19
  78.6 5.8 copy-start.2
  79.5 7.7 %collective-permute-start.4 = (f32[2,256,128]{2,1,0:T(8,128)S(1)}, f32[2,256,128]{2,1,0:T(8,128)S(1)}, u32[]{:S(2)}, u32[]{:S(2)}) collective-permute-start(f32[2,256,128]{2,1,0:T(8,128)S(1)} %fusion.74), channel_id=1, source_target_pairs={{0,504},{8,0},{16,8},{24,16},{32,24},{40,32},{48,40},{56,48},{64,5... | collective-permute-start | bytes 786440 | tf_op jit(solution)/shard_map/ppermute | solution.py:19
  84.5 9.6 %copy-start.12 = (bf16[16,1024]{1,0:T(8,128)(2,1)S(1)}, bf16[16,1024]{1,0:T(8,128)(2,1)}, u32[]{:S(2)}) copy-start(bf16[16,1024]{1,0:T(8,128)(2,1)} %param.18) | copy-start | bytes 98308
  84.8 10.3 %copy-start.14 = (bf16[2,16,128]{2,1,0:T(8,128)(2,1)S(1)}, bf16[2,16,128]{2,1,0:T(8,128)(2,1)}, u32[]{:S(2)}) copy-start(bf16[2,16,128]{2,1,0:T(8,128)(2,1)} %param.19) | copy-start | bytes 24580
  87.2 7.9 %collective-permute-start.5 = (f32[2,256,128]{2,1,0:T(8,128)S(1)}, f32[2,256,128]{2,1,0:T(8,128)S(1)}, u32[]{:S(2)}, u32[]{:S(2)}) collective-permute-start(f32[2,256,128]{2,1,0:T(8,128)S(1)} %fusion.71), channel_id=1, source_target_pairs={{0,504},{8,0},{16,8},{24,16},{32,24},{40,32},{48,40},{56,48},{64,5... | collective-permute-start | bytes 786440 | tf_op jit(solution)/shard_map/ppermute | solution.py:19
  95.2 659.8 %copy-start.7 = (bf16[2,256,128]{2,1,0:T(8,128)(2,1)}, bf16[2,256,128]{2,1,0:T(8,128)(2,1)S(1)}, u32[]{:S(2)}) copy-start(bf16[2,256,128]{2,1,0:T(8,128)(2,1)S(1)} %fusion.76) | copy-start | bytes 393220
Sparse Core Ops, SparseCore 0:
  350.0 401.8 all-reduce.3
where the time goes:
time: 763 us; the launch traced here: 762 us
  waiting for transfers between devices  418 us (55%)
  blocking collectives  252 us (33%)
  matrix products  39 us (5%)
  starting transfers between devices  27.4 us (4%)
  between operations  14.5 us (2%)
    psum x1, waiting for transfers between devices, per_device(): lax.psum((down_term, up_q_term, up_kv_term), 'seq')  400 us
    psum x1, blocking collectives, per_device(): lax.psum((down_term, up_q_term, up_kv_term), 'seq')  217 us
    psum x1, blocking collectives, per_device(): up_backward_term = lax.psum(up_part, 'head')  35.7 us
    ppermute x6, starting transfers between devices, shifted(): lax.ppermute(shard, axis, [(i, (i + by) % devices) for i in range(devices)])  27.3 us
    ppermute x6, waiting for transfers between devices, shifted(): lax.ppermute(shard, axis, [(i, (i + by) % devices) for i in range(devices)])  18 us
  transfers between devices with their start and end apart: 7, of which 7 were waited for; matrix products, arithmetic and copies ran while one was open for 1% of the time, Pallas kernels for 0%

commit v1 on v0

v1 whole, which is shorter than its diff:
```python
import functools
import math

import jax
import jax.numpy as jnp
from jax import lax
from jax.experimental import pallas as pl
from jax.experimental.pallas import tpu as pltpu
from jax.sharding import PartitionSpec as P

HEAD_SIZE = 128
GROUP = 1024
RANK = 16
QUAD = 4
UNITS = 16
LOG2E = 1.4426950408889634
BIG = 1e30
ADAPTER_SCALE = 2.0

MESH = pl.DeviceIdType.MESH
F32 = jnp.float32
BF16 = jnp.bfloat16


def dot_nn(a, b):
    return lax.dot_general(a, b, (((1,), (0,)), ((), ())), preferred_element_type=F32)


def dot_nt(a, b):
    return lax.dot_general(a, b, (((1,), (1,)), ((), ())), preferred_element_type=F32)


def kernel(
    seq_count,
    head_count,
    q_hbm, k_hbm, v_hbm, do_hbm, rs_hbm, flags, x_hbm, wd_hbm, wq_hbm, wkv_hbm,
    kv_out, up_out, g_out, c_out,
    q_v, do_v, x_v, wd_v, wq_v, wkv_v, rs_v,
    kwin, vwin, k_t, probs, dscores, own_kv, kv_send, kv_recv,
    down_send, down_recv, down_low, upq_send, upq_recv, upkv_send, upkv_recv,
    g_full, g_send, g_recv, c_full, c_recv, units, z_recv, cz,
    load_sem, win_send, win_recv, down_ss, down_rs, upq_ss, upq_rs, upkv_ss, upkv_rs,
    kv_ss, kv_rs, quad_ss, quad_rs, quadc_ss, quadc_rs, z_ss, z_rs, cz_ss, cz_rs,
    ag_ss, ag_rs, fin_ss, fin_rs, finc_ss, finc_rs,
):
    tokens = q_v.shape[0]
    heads = q_v.shape[1] // HEAD_SIZE
    nz = seq_count // QUAD
    per_owner = UNITS // nz
    s = lax.axis_index("seq")
    hd = lax.axis_index("head")
    zi = s // QUAD
    b = s % QUAD
    core = s % 2
    x_lo = b // 2
    scale = HEAD_SIZE ** -0.5
    multiplier = ADAPTER_SCALE / math.sqrt(tokens * seq_count)

    def seq_at(by):
        return lax.rem(s + by + seq_count, seq_count)

    def head_at(by):
        return lax.rem(hd + by + head_count, head_count)

    def z_at(by):
        return lax.rem(zi + by + nz, nz)

    def quad_at(by):
        return lax.rem(b + by + QUAD, QUAD)

    def z_peer(by):
        return z_at(by) * QUAD + b

    def quad_peer(by):
        return zi * QUAD + quad_at(by)

    loads = [
        pltpu.make_async_copy(src, dst, load_sem.at[i])
        for i, (src, dst) in enumerate([
            (k_hbm, kwin.at[3]), (v_hbm, vwin.at[3]), (x_hbm, x_v), (wd_hbm, wd_v), (q_hbm, q_v),
            (do_hbm, do_v), (rs_hbm, rs_v), (wq_hbm, wq_v), (wkv_hbm, wkv_v),
        ])
    ]
    for copy in loads:
        copy.start()

    barrier = pltpu.get_barrier_semaphore()
    near = [-3, -2, -1, 1, 2, 3]
    for by in near:
        pl.semaphore_signal(barrier, inc=1, device_id={"seq": seq_at(by)}, device_id_type=MESH)
    for by in range(1, head_count):
        pl.semaphore_signal(barrier, inc=1, device_id={"head": head_at(by)}, device_id_type=MESH)

    def greet(by, _):
        pl.semaphore_signal(barrier, inc=1, device_id={"seq": z_peer(by)}, device_id_type=MESH)
        return 0

    lax.fori_loop(1, nz, greet, 0)
    pl.semaphore_wait(barrier, len(near) + head_count - 1 + nz - 1)

    def window_copy(which, by):
        src, dst = ((k_hbm, kwin), (v_hbm, vwin))[which]
        return pltpu.make_async_remote_copy(
            src_ref=src, dst_ref=dst.at[3 - by],
            send_sem=win_send.at[which, by], recv_sem=win_recv.at[which, 3 - by],
            device_id={"seq": seq_at(by)}, device_id_type=MESH,
        )

    for which in range(2):
        window_copy(which, 1).start()
        window_copy(which, 2).start()

        @pl.when(core == 0)
        def _():
            window_copy(which, 3).start()

    def head_copy(src, dst, ss, rs, by):
        return pltpu.make_async_remote_copy(
            src_ref=src, dst_ref=dst.at[by], send_sem=ss.at[by], recv_sem=rs.at[by],
            device_id={"head": head_at(by)}, device_id_type=MESH,
        )

    loads[2].wait()
    loads[3].wait()
    down_part = dot_nt(wd_v[...], x_v[...])
    down_send[...] = down_part.astype(BF16)
    for by in range(1, head_count):
        head_copy(down_send, down_recv, down_ss, down_rs, by).start()

    for i in (0, 1, 4, 5, 6, 7, 8):
        loads[i].wait()

    row_id = lax.broadcasted_iota(jnp.int32, (tokens, tokens), 0)
    col_id = lax.broadcasted_iota(jnp.int32, (tokens, tokens), 1)
    causal = jnp.where(row_id <= col_id, 0.0, -BIG).astype(F32)
    want = (1 - x_lo).astype(F32)
    even = (1 - core).astype(F32)
    c2 = scale * LOG2E

    def head_cols(ref, h):
        return ref[:, pl.ds(pl.multiple_of(h * HEAD_SIZE, HEAD_SIZE), HEAD_SIZE)]

    def attention(slots):
        def rows(j):
            return pl.ds(j * tokens, tokens)

        for j in slots:
            if j < 3:
                window_copy(0, 3 - j).wait_recv()
            k_t[:, j * tokens : (j + 1) * tokens] = kwin[j].astype(F32).T.astype(BF16)

        def forward(h, _):
            q = head_cols(q_v, h)
            differs = flags[h].astype(F32) - want
            far = differs * differs * BIG
            bias = {0: far, 1: far, 2: far * even, 3: 0.0}
            score = {}
            top = None
            for j in slots:
                score[j] = dot_nt(kwin[j], q)
                if j == 3:
                    score[j] = score[j] + causal
                high = jnp.max(score[j], axis=0, keepdims=True) - bias[j]
                top = high if top is None else jnp.maximum(top, high)
            weight = {}
            total = None
            for j in slots:
                weight[j] = jnp.exp2(score[j] * c2 - (top * c2 + bias[j]))
                part = jnp.sum(weight[j], axis=0, keepdims=True)
                total = part if total is None else total + part
            inverse = 1.0 / total
            for j in slots:
                probs[h, rows(j), :] = (weight[j] * inverse).astype(BF16)
            return 0

        lax.fori_loop(0, heads, forward, 0)

        for j in slots:
            if j < 3:
                window_copy(1, 3 - j).wait_recv()

            def backward(h, acc):
                dk, dv = acc
                q = head_cols(q_v, h)
                do = head_cols(do_v, h)
                p = probs[h, rows(j), :]
                dp = dot_nt(vwin[j], do)
                ds = (p.astype(F32) * (dp - rs_v[pl.ds(h, 1), :])).astype(BF16)
                dscores[h, rows(j), :] = ds
                return dk + dot_nn(ds, q), dv + dot_nn(p, do)

            zero = jnp.zeros((tokens, HEAD_SIZE), F32)
            dk, dv = lax.fori_loop(0, heads, backward, (zero, zero))
            if j == 3:
                own_kv[0] = dk * scale
                own_kv[1] = dv
            else:
                kv_send[j, 0] = (dk * scale).astype(BF16)
                kv_send[j, 1] = dv.astype(BF16)
                grad_copy(3 - j).start()

    def grad_copy(by):
        return pltpu.make_async_remote_copy(
            src_ref=kv_send.at[3 - by], dst_ref=kv_recv.at[by],
            send_sem=kv_ss.at[by], recv_sem=kv_rs.at[by],
            device_id={"seq": seq_at(-by)}, device_id_type=MESH,
        )

    @pl.when(core == 1)
    def _():
        attention((0, 1, 2, 3))

    @pl.when(core == 0)
    def _():
        attention((1, 2, 3))

    down = down_part
    for by in range(1, head_count):
        head_copy(down_send, down_recv, down_ss, down_rs, by).wait_recv()
        down = down + down_recv[by].astype(F32)
    down_low[...] = down.astype(BF16)

    def query_grads(first):
        def one(h, acc):
            dq = (dot_nn(k_t[:, first:], dscores[h, first:, :]) * scale).astype(BF16)
            a = dot_nt(down_low[:RANK, :], dq)
            g_col = pl.ds(pl.multiple_of((h % 2) * HEAD_SIZE, HEAD_SIZE), HEAD_SIZE)
            g_full[h // 2, 3 * RANK :, g_col] = a
            return acc + dot_nn(head_cols(wq_v, h), dq)

        upq_send_f32 = lax.fori_loop(0, heads, one, jnp.zeros((RANK, tokens), F32))
        upq_send[...] = upq_send_f32.astype(BF16)

    @pl.when(core == 1)
    def _():
        query_grads(0)

    @pl.when(core == 0)
    def _():
        query_grads(tokens)

    for by in range(1, head_count):
        head_copy(upq_send, upq_recv, upq_ss, upq_rs, by).start()

    grad_copy(1).wait_recv()
    grad_copy(2).wait_recv()

    @pl.when(core == 0)
    def _():
        grad_copy(3).wait_recv()
        own_kv[...] = own_kv[...] + kv_recv[3].astype(F32)

    dkv = (own_kv[...] + kv_recv[1].astype(F32) + kv_recv[2].astype(F32)).astype(BF16)
    kv_out[...] = dkv
    for c in range(2):
        upkv_send[c * RANK : (c + 1) * RANK, :] = dot_nt(
            wkv_v[c * RANK : (c + 1) * RANK, :], dkv[c]
        ).astype(BF16)
    for by in range(1, head_count):
        head_copy(upkv_send, upkv_recv, upkv_ss, upkv_rs, by).start()
    for c in range(2):
        part = dot_nn(down_low[(c + 1) * RANK : (c + 2) * RANK, :], dkv[c])
        c_full[2 * c] = part[:8]
        c_full[2 * c + 1] = part[8:]

    up = upq_send[...].astype(F32)
    for by in range(1, head_count):
        head_copy(upq_send, upq_recv, upq_ss, upq_rs, by).wait_recv()
        up = up + upq_recv[by].astype(F32)
    up_out[:RANK, :] = up.astype(BF16)
    up = upkv_send[...].astype(F32)
    for by in range(1, head_count):
        head_copy(upkv_send, upkv_recv, upkv_ss, upkv_rs, by).wait_recv()
        up = up + upkv_recv[by].astype(F32)
    up_out[RANK:, :] = up.astype(BF16)
    width = x_v.shape[1] // QUAD
    for c in range(QUAD):
        g_full[c, : 3 * RANK, :] = dot_nn(up_out[...], x_v[:, c * width : (c + 1) * width])
    g_send[...] = g_full[...].astype(BF16)

    def quad_copy(by):
        return pltpu.make_async_remote_copy(
            src_ref=g_send.at[quad_at(by)], dst_ref=g_recv.at[by],
            send_sem=quad_ss.at[by], recv_sem=quad_rs.at[by],
            device_id={"seq": quad_peer(by)}, device_id_type=MESH,
        )

    def quad_copy_c(by):
        return pltpu.make_async_remote_copy(
            src_ref=c_full.at[quad_at(by)], dst_ref=c_recv.at[by],
            send_sem=quadc_ss.at[by], recv_sem=quadc_rs.at[by],
            device_id={"seq": quad_peer(by)}, device_id_type=MESH,
        )

    for by in range(1, QUAD):
        quad_copy(by).start()
        quad_copy_c(by).start()
    g = g_full[b]
    c_sum = c_full[b]
    for by in range(1, QUAD):
        quad_copy(by).wait_recv()
        quad_copy_c(by).wait_recv()
        g = g + g_recv[by].astype(F32)
        c_sum = c_sum + c_recv[by]
    for u in range(UNITS):
        r, col = u // 2, u % 2
        units[u // per_owner, u % per_owner] = g[r * 8 : r * 8 + 8, col * 128 : col * 128 + 128]
    cz[zi] = c_sum

    def z_copy(by):
        return pltpu.make_async_remote_copy(
            src_ref=units.at[z_at(by)], dst_ref=z_recv.at[by],
            send_sem=z_ss.at[by], recv_sem=z_rs.at[by],
            device_id={"seq": z_peer(by)}, device_id_type=MESH,
        )

    def cz_copy(by, slot):
        return pltpu.make_async_remote_copy(
            src_ref=cz.at[slot], dst_ref=cz.at[slot],
            send_sem=cz_ss.at[by], recv_sem=cz_rs.at[slot],
            device_id={"seq": z_peer(by)}, device_id_type=MESH,
        )

    def send_z(by, _):
        z_copy(by).start()
        return 0

    def send_cz(by, _):
        cz_copy(by, zi).start()
        return 0

    lax.fori_loop(1, nz, send_z, 0)
    lax.fori_loop(1, nz, send_cz, 0)

    def add_z(by, acc):
        z_copy(by).wait_recv()
        return acc + z_recv[by]

    total = lax.fori_loop(1, nz, add_z, units[zi]) * multiplier

    def unit_slice(u, quad):
        return (
            pl.ds(pl.multiple_of((u // 2) * 8, 8), 8),
            pl.ds(pl.multiple_of(quad * width + (u % 2) * 128, 128), 128),
        )

    for i in range(per_owner):
        at = unit_slice(zi * per_owner + i, b)
        g_out[at[0], at[1]] = total[i]

    def gather_copy(by, owner, i):
        u = owner * per_owner + i
        at = unit_slice(u, b)
        return pltpu.make_async_remote_copy(
            src_ref=g_out.at[at[0], at[1]], dst_ref=g_out.at[at[0], at[1]],
            send_sem=ag_ss.at[by * per_owner + i], recv_sem=ag_rs.at[u],
            device_id={"seq": z_peer(by)}, device_id_type=MESH,
        )

    def send_gather(by, _):
        for i in range(per_owner):
            gather_copy(by, zi, i).start()
        return 0

    lax.fori_loop(1, nz, send_gather, 0)

    def wait_cz(by, _):
        cz_copy(by, z_at(-by)).wait_recv()
        return 0

    lax.fori_loop(1, nz, wait_cz, 0)
    c_total = jnp.sum(cz[...], axis=0) * multiplier
    c_at = pl.ds(pl.multiple_of(b * 8, 8), 8)
    c_out[c_at, :] = c_total

    def wait_gather(by, _):
        for i in range(per_owner):
            gather_copy(by, z_at(-by), i).wait_recv()
        return 0

    lax.fori_loop(1, nz, wait_gather, 0)

    def final_copy(by, quad):
        cols = pl.ds(pl.multiple_of(quad * width, 128), width)
        return pltpu.make_async_remote_copy(
            src_ref=g_out.at[:, cols], dst_ref=g_out.at[:, cols],
            send_sem=fin_ss.at[by], recv_sem=fin_rs.at[by],
            device_id={"seq": quad_peer(by)}, device_id_type=MESH,
        )

    def final_copy_c(by, quad):
        at = pl.ds(pl.multiple_of(quad * 8, 8), 8)
        return pltpu.make_async_remote_copy(
            src_ref=c_out.at[at, :], dst_ref=c_out.at[at, :],
            send_sem=finc_ss.at[by], recv_sem=finc_rs.at[by],
            device_id={"seq": quad_peer(by)}, device_id_type=MESH,
        )

    for by in range(1, QUAD):
        final_copy(by, b).start()
        final_copy_c(by, b).start()

    for which in range(2):
        window_copy(which, 1).wait_send()
        window_copy(which, 2).wait_send()

        @pl.when(core == 0)
        def _():
            window_copy(which, 3).wait_send()

    grad_copy(1).wait_send()
    grad_copy(2).wait_send()

    @pl.when(core == 1)
    def _():
        grad_copy(3).wait_send()

    for by in range(1, head_count):
        head_copy(down_send, down_recv, down_ss, down_rs, by).wait_send()
        head_copy(upq_send, upq_recv, upq_ss, upq_rs, by).wait_send()
        head_copy(upkv_send, upkv_recv, upkv_ss, upkv_rs, by).wait_send()
    for by in range(1, QUAD):
        quad_copy(by).wait_send()
        quad_copy_c(by).wait_send()

    def wait_z(by, _):
        z_copy(by).wait_send()
        cz_copy(by, zi).wait_send()
        for i in range(per_owner):
            gather_copy(by, zi, i).wait_send()
        return 0

    lax.fori_loop(1, nz, wait_z, 0)
    for by in range(1, QUAD):
        final_copy(by, quad_at(-by)).wait_recv()
        final_copy_c(by, quad_at(-by)).wait_recv()
        final_copy(by, b).wait_send()
        final_copy_c(by, b).wait_send()


def per_device(
    queries, layer_key_rows, layer_value_rows, output_gradient, output_row_sums,
    shifted_head_flags, inputs, adapter_down_weight, query_up_weight, key_value_up_weight,
):
    seq_count = lax.axis_size("seq")
    head_count = lax.axis_size("head")
    tokens, columns = queries.shape
    heads = columns // HEAD_SIZE
    width = inputs.shape[1]
    nz = seq_count // QUAD
    per_owner = UNITS // nz
    flat_down = adapter_down_weight.reshape(3 * RANK, width)
    flat_kv_up = key_value_up_weight.reshape(2 * RANK, HEAD_SIZE)
    vmem = pltpu.VMEM
    sem = pltpu.SemaphoreType.DMA
    anywhere = pl.BlockSpec(memory_space=pl.ANY)
    in_vmem = pl.BlockSpec(memory_space=pltpu.VMEM)
    kv_out, up_out, g_out, c_out = pl.pallas_call(
        functools.partial(kernel, seq_count, head_count),
        out_shape=(
            jax.ShapeDtypeStruct((2, tokens, HEAD_SIZE), BF16),
            jax.ShapeDtypeStruct((3 * RANK, tokens), BF16),
            jax.ShapeDtypeStruct((4 * RANK, width), F32),
            jax.ShapeDtypeStruct((2 * RANK, HEAD_SIZE), F32),
        ),
        in_specs=[anywhere] * 5 + [pl.BlockSpec(memory_space=pltpu.SMEM)] + [anywhere] * 4,
        out_specs=(in_vmem,) * 4,
        scratch_shapes=[
            vmem((tokens, columns), BF16),
            vmem((tokens, columns), BF16),
            vmem((tokens, width), BF16),
            vmem((3 * RANK, width), BF16),
            vmem((RANK, columns), BF16),
            vmem((2 * RANK, HEAD_SIZE), BF16),
            vmem((heads, tokens), F32),
            vmem((4, tokens, HEAD_SIZE), BF16),
            vmem((4, tokens, HEAD_SIZE), BF16),
            vmem((HEAD_SIZE, 4 * tokens), BF16),
            vmem((heads, 4 * tokens, tokens), BF16),
            vmem((heads, 4 * tokens, tokens), BF16),
            vmem((2, tokens, HEAD_SIZE), F32),
            vmem((3, 2, tokens, HEAD_SIZE), BF16),
            vmem((4, 2, tokens, HEAD_SIZE), BF16),
            vmem((3 * RANK, tokens), BF16),
            vmem((head_count, 3 * RANK, tokens), BF16),
            vmem((3 * RANK, tokens), BF16),
            vmem((RANK, tokens), BF16),
            vmem((head_count, RANK, tokens), BF16),
            vmem((2 * RANK, tokens), BF16),
            vmem((head_count, 2 * RANK, tokens), BF16),
            vmem((QUAD, 4 * RANK, width // QUAD), F32),
            vmem((QUAD, 4 * RANK, width // QUAD), BF16),
            vmem((QUAD, 4 * RANK, width // QUAD), BF16),
            vmem((QUAD, 8, HEAD_SIZE), F32),
            vmem((QUAD, 8, HEAD_SIZE), F32),
            vmem((nz, per_owner, 8, 128), F32),
            vmem((nz, per_owner, 8, 128), F32),
            vmem((nz, 8, HEAD_SIZE), F32),
            sem((9,)),
            sem((2, 4)), sem((2, 4)),
            sem((head_count,)), sem((head_count,)),
            sem((head_count,)), sem((head_count,)),
            sem((head_count,)), sem((head_count,)),
            sem((4,)), sem((4,)),
            sem((QUAD,)), sem((QUAD,)),
            sem((QUAD,)), sem((QUAD,)),
            sem((nz,)), sem((nz,)),
            sem((nz,)), sem((nz,)),
            sem((UNITS,)), sem((UNITS,)),
            sem((QUAD,)), sem((QUAD,)),
            sem((QUAD,)), sem((QUAD,)),
        ],
        compiler_params=pltpu.CompilerParams(
            collective_id=0, has_side_effects=True, vmem_limit_bytes=48 * 1024 * 1024
        ),
    )(
        queries, layer_key_rows, layer_value_rows, output_gradient, output_row_sums,
        shifted_head_flags, inputs, flat_down, query_up_weight, flat_kv_up,
    )
    grad_inputs = (
        ADAPTER_SCALE
        * lax.dot_general(
            up_out, flat_down, (((0,), (0,)), ((), ())), preferred_element_type=F32
        )
    ).astype(BF16)
    return (
        grad_inputs,
        kv_out,
        g_out[: 3 * RANK].reshape(3, RANK, width),
        g_out[3 * RANK :],
        c_out.reshape(2, RANK, HEAD_SIZE),
    )


def solution(mesh):
    placed = (
        P("seq", "head"),
        P("seq", "head"),
        P("seq", "head"),
        P("seq", "head"),
        P("head", "seq"),
        P("head"),
        P("seq", "head"),
        P(None, None, "head"),
        P(None, "head"),
        P(None, None, "head"),
    )
    return jax.shard_map(
        per_device,
        mesh=mesh,
        in_specs=placed,
        out_specs=(
            P("seq", "head"),
            P(None, "seq", "head"),
            P(None, None, "head"),
            P(None, "head"),
            P(None, None, "head"),
        ),
        check_vma=False,
    )
```

time: 763 us -> 89.7 us (0.12)
  waiting for transfers between devices: 418 us -> 0 us
  blocking collectives: 252 us -> 0 us
  Pallas kernels: 0 us -> 76.3 us
  matrix products: 39 us -> 1.11 us
  starting transfers between devices: 27.4 us -> 0 us
  between operations: 14.5 us -> 0.66 us
    psum x1 -> x0, waiting for transfers between devices: 400 us -> none  [per_device(): lax.psum((down_term, up_q_term, up_kv_term), 'seq')]
    psum x2 -> x0, blocking collectives: 252 us -> none  [the longest x1 217 us: per_device(): lax.psum((down_term, up_q_term, up_kv_term), 'seq')]
    pallas_call x0 -> x1, Pallas kernels: none -> 76.3 us  [per_device(): pl.pallas_call(functools.partial(kernel, seq_count, head_count), out_shap...]
    ppermute x6 -> x0, starting transfers between devices: 27.3 us -> none  [shifted(): lax.ppermute(shard, axis, [(i, (i + by) % devices) for i in range(devices)])]
    dot_general x25 -> x1, matrix products: 27.7 us -> 1.11 us  [per_device(): lax.dot_general(up_out, flat_down, (((0,), (0,)), ((), ())), preferred_el...]
    ppermute x6 -> x0, waiting for transfers between devices: 18 us -> none  [shifted(): lax.ppermute(shard, axis, [(i, (i + by) % devices) for i in range(devices)])]
    sub x4 -> x0, matrix products: 11.3 us -> none  [block_backward(): weights = jnp.where(visible, jnp.exp(scores - row_max), 0.0)]
  transfers between devices with their start and end apart: 7 -> 0, of which waited for: 7 -> 0; matrix products, arithmetic and copies ran while one was open for 1% -> 0% of each run, Pallas kernels for 0% -> 0%
where the time goes in v1:
time: 89.7 us; the launch traced here: 89.2 us
  Pallas kernels  76.3 us (85%)
  local copies, waits for them, and re-layouts  11.1 us (12%)
  matrix products  1.11 us (1%)
    pallas_call x1, Pallas kernels, per_device(): pl.pallas_call(functools.partial(kernel, seq_count, head_count), out_shap...  76.3 us
    unnamed x22, local copies, waits for them, and re-layouts  9.75 us

profile of v1, /device:TPU:1, one launch (start us, length us, event | category | flops | bytes accessed | tf_op | source)
XLA Modules:
  0.0 89.2 jit_solution(9770037851421298322)
XLA Ops:
  0.6 0.0 copy-start.9
  0.6 0.6 copy-done.9
  1.3 0.0 copy-start
  1.3 1.0 %copy-done = bf16[256,1024]{1,0:T(8,128)(2,1)S(1)} copy-done((bf16[256,1024]{1,0:T(8,128)(2,1)S(1)}, bf16[256,1024]{1,0:T(8,128)(2,1)}, u32[]{:S(2)}) %copy-start) | copy-done | bytes 524312
  2.3 0.0 copy-start.1
  2.3 1.0 %copy-done.1 = bf16[256,1024]{1,0:T(8,128)(2,1)S(1)} copy-done((bf16[256,1024]{1,0:T(8,128)(2,1)S(1)}, bf16[256,1024]{1,0:T(8,128)(2,1)}, u32[]{:S(2)}) %copy-start.1) | copy-done | bytes 524312
  3.4 0.0 copy-start.2
  3.4 1.0 %copy-done.2 = bf16[256,1024]{1,0:T(8,128)(2,1)S(1)} copy-done((bf16[256,1024]{1,0:T(8,128)(2,1)S(1)}, bf16[256,1024]{1,0:T(8,128)(2,1)}, u32[]{:S(2)}) %copy-start.2) | copy-done | bytes 524312
  4.4 0.0 copy-start.3
  4.4 0.9 copy-done.3
  5.3 0.0 copy-start.4
  5.3 0.8 copy-done.4
  6.2 0.0 copy-start.5
  6.2 0.8 copy-done.5
  7.0 0.0 copy-start.6
  7.0 0.8 copy-done.6
  7.7 0.0 copy-start.7
  7.8 0.7 copy-done.7
  8.4 0.0 copy-start.8
  8.4 0.7 copy-done.8
  9.1 76.3 %shard_map.137 = (bf16[2,256,128]{2,1,0:T(8,128)(2,1)S(1)}, bf16[48,256]{1,0:T(8,128)(2,1)S(1)}, f32[64,1024]{1,0:T(8,128)S(1)}, f32[32,128]{1,0:T(8,128)S(1)}) custom-call(bf16[256,1024]{1,0:T(8,128)(2,1)S(1)} %copy-done, bf16[256,128]{1,0:T(8,128)(2,1)S(1)} %copy-done.4, bf16[256,128]{1,0:T(8,128)(2,1)S(1)} %copy-done.5, bf16[256,1024]{1,0:T(8,128)(2,1)S(1)} %copy-done.1, ...), custom_call_target="tpu_custom_call" | custom-call | tf_op jit(solution)/shard_map/pallas_call | solution.py:458
  85.5 0.6 slice.7
  86.1 0.7 slice.6
  86.8 1.1 %fusion = bf16[256,1024]{1,0:T(8,128)(2,1)} fusion(bf16[48,256]{1,0:T(8,128)(2,1)S(1)} %get-tuple-element.9, bf16[48,1024]{1,0:T(8,128)(2,1)S(1)} %bitcast.7), kind=kOutput, calls=%fused_computation.1 | convolution fusion | flops 25690112 | bytes 647168 | tf_op jit(solution)/shard_map/dot_general | solution.py:522
  87.9 0.7 copy.17
  88.6 0.6 copy.18
Async XLA Ops:
  0.6 0.7 copy-start.9
  1.3 1.0 %copy-start = (bf16[256,1024]{1,0:T(8,128)(2,1)S(1)}, bf16[256,1024]{1,0:T(8,128)(2,1)}, u32[]{:S(2)}) copy-start(bf16[256,1024]{1,0:T(8,128)(2,1)} %q_hbm.1) | copy-start | bytes 1572868
  2.3 1.0 %copy-start.1 = (bf16[256,1024]{1,0:T(8,128)(2,1)S(1)}, bf16[256,1024]{1,0:T(8,128)(2,1)}, u32[]{:S(2)}) copy-start(bf16[256,1024]{1,0:T(8,128)(2,1)} %do_hbm.1) | copy-start | bytes 1572868
  3.4 1.0 %copy-start.2 = (bf16[256,1024]{1,0:T(8,128)(2,1)S(1)}, bf16[256,1024]{1,0:T(8,128)(2,1)}, u32[]{:S(2)}) copy-start(bf16[256,1024]{1,0:T(8,128)(2,1)} %x_hbm.1) | copy-start | bytes 1572868
  4.4 0.9 %copy-start.3 = (bf16[3,16,1024]{2,1,0:T(8,128)(2,1)S(1)}, bf16[3,16,1024]{2,1,0:T(8,128)(2,1)}, u32[]{:S(2)}) copy-start(bf16[3,16,1024]{2,1,0:T(8,128)(2,1)} %param.17) | copy-start | bytes 294916
  5.3 0.8 copy-start.4
  6.2 0.8 copy-start.5
  7.0 0.8 copy-start.6
  7.7 0.7 copy-start.7
  8.4 0.7 copy-start.8

commit v2 on v1

--- a/solution.py
+++ b/solution.py
@@ -16,6 +16,7 @@
 LOG2E = 1.4426950408889634
 BIG = 1e30
 ADAPTER_SCALE = 2.0
+VMEM_BYTES = 63 * 1024 * 1024
 
 MESH = pl.DeviceIdType.MESH
 F32 = jnp.float32
@@ -34,8 +35,8 @@
     seq_count,
     head_count,
     q_hbm, k_hbm, v_hbm, do_hbm, rs_hbm, flags, x_hbm, wd_hbm, wq_hbm, wkv_hbm,
-    kv_out, up_out, g_out, c_out,
-    q_v, do_v, x_v, wd_v, wq_v, wkv_v, rs_v,
+    kv_out, x_out, g_out, c_out,
+    up_out, q_v, do_v, x_v, wd_v, wq_v, wkv_v, rs_v,
     kwin, vwin, k_t, probs, dscores, own_kv, kv_send, kv_recv,
     down_send, down_recv, down_low, upq_send, upq_recv, upkv_send, upkv_recv,
     g_full, g_send, g_recv, c_full, c_recv, units, z_recv, cz,
@@ -74,6 +75,8 @@
     def quad_peer(by):
         return zi * QUAD + quad_at(by)
 
+    pending = []
+
     loads = [
         pltpu.make_async_copy(src, dst, load_sem.at[i])
         for i, (src, dst) in enumerate([
@@ -114,6 +117,17 @@
         def _():
             window_copy(which, 3).start()
 
+    def window_sent():
+        for which in range(2):
+            window_copy(which, 1).wait_send()
+            window_copy(which, 2).wait_send()
+
+            @pl.when(core == 0)
+            def _():
+                window_copy(which, 3).wait_send()
+
+    pending.append(window_sent)
+
     def head_copy(src, dst, ss, rs, by):
         return pltpu.make_async_remote_copy(
             src_ref=src, dst_ref=dst.at[by], send_sem=ss.at[by], recv_sem=rs.at[by],
@@ -126,6 +140,15 @@
     down_send[...] = down_part.astype(BF16)
     for by in range(1, head_count):
         head_copy(down_send, down_recv, down_ss, down_rs, by).start()
+
+    def head_sent(*args):
+        def wait():
+            for by in range(1, head_count):
+                head_copy(*args, by).wait_send()
+
+        pending.append(wait)
+
+    head_sent(down_send, down_recv, down_ss, down_rs)
 
     for i in (0, 1, 4, 5, 6, 7, 8):
         loads[i].wait()
@@ -214,6 +237,16 @@
     def _():
         attention((1, 2, 3))
 
+    def grads_sent():
+        grad_copy(1).wait_send()
+        grad_copy(2).wait_send()
+
+        @pl.when(core == 1)
+        def _():
+            grad_copy(3).wait_send()
+
+    pending.append(grads_sent)
+
     down = down_part
     for by in range(1, head_count):
         head_copy(down_send, down_recv, down_ss, down_rs, by).wait_recv()
@@ -241,6 +274,7 @@
 
     for by in range(1, head_count):
         head_copy(upq_send, upq_recv, upq_ss, upq_rs, by).start()
+    head_sent(upq_send, upq_recv, upq_ss, upq_rs)
 
     grad_copy(1).wait_recv()
     grad_copy(2).wait_recv()
@@ -258,10 +292,12 @@
         ).astype(BF16)
     for by in range(1, head_count):
         head_copy(upkv_send, upkv_recv, upkv_ss, upkv_rs, by).start()
+    head_sent(upkv_send, upkv_recv, upkv_ss, upkv_rs)
     for c in range(2):
         part = dot_nn(down_low[(c + 1) * RANK : (c + 2) * RANK, :], dkv[c])
         c_full[2 * c] = part[:8]
         c_full[2 * c + 1] = part[8:]
+
 
     up = upq_send[...].astype(F32)
     for by in range(1, head_count):
@@ -278,6 +314,7 @@
         g_full[c, : 3 * RANK, :] = dot_nn(up_out[...], x_v[:, c * width : (c + 1) * width])
     g_send[...] = g_full[...].astype(BF16)
 
+
     def quad_copy(by):
         return pltpu.make_async_remote_copy(
             src_ref=g_send.at[quad_at(by)], dst_ref=g_recv.at[by],
@@ -295,6 +332,19 @@
     for by in range(1, QUAD):
         quad_copy(by).start()
         quad_copy_c(by).start()
+
+    def quad_sent():
+        for by in range(1, QUAD):
+            quad_copy(by).wait_send()
+            quad_copy_c(by).wait_send()
+
+    pending.append(quad_sent)
+    for c in range(QUAD):
+        cols = slice(c * width, (c + 1) * width)
+        part = lax.dot_general(
+            up_out[...], wd_v[:, cols], (((0,), (0,)), ((), ())), preferred_element_type=F32
+        )
+        x_out[:, cols] = (ADAPTER_SCALE * part).astype(BF16)
     g = g_full[b]
     c_sum = c_full[b]
     for by in range(1, QUAD):
@@ -307,6 +357,7 @@
         units[u // per_owner, u % per_owner] = g[r * 8 : r * 8 + 8, col * 128 : col * 128 + 128]
     cz[zi] = c_sum
 
+
     def z_copy(by):
         return pltpu.make_async_remote_copy(
             src_ref=units.at[z_at(by)], dst_ref=z_recv.at[by],
@@ -332,11 +383,19 @@
     lax.fori_loop(1, nz, send_z, 0)
     lax.fori_loop(1, nz, send_cz, 0)
 
+    def wait_z(by, _):
+        z_copy(by).wait_send()
+        cz_copy(by, zi).wait_send()
+        return 0
+
+    pending.append(lambda: lax.fori_loop(1, nz, wait_z, 0))
+
     def add_z(by, acc):
         z_copy(by).wait_recv()
         return acc + z_recv[by]
 
     total = lax.fori_loop(1, nz, add_z, units[zi]) * multiplier
+
 
     def unit_slice(u, quad):
         return (
@@ -364,6 +423,13 @@
 
     lax.fori_loop(1, nz, send_gather, 0)
 
+    def wait_gather_sent(by, _):
+        for i in range(per_owner):
+            gather_copy(by, zi, i).wait_send()
+        return 0
+
+    pending.append(lambda: lax.fori_loop(1, nz, wait_gather_sent, 0))
+
     def wait_cz(by, _):
         cz_copy(by, z_at(-by)).wait_recv()
         return 0
@@ -380,6 +446,7 @@
 
     lax.fori_loop(1, nz, wait_gather, 0)
 
+
     def final_copy(by, quad):
         cols = pl.ds(pl.multiple_of(quad * width, 128), width)
         return pltpu.make_async_remote_copy(
@@ -400,42 +467,38 @@
         final_copy(by, b).start()
         final_copy_c(by, b).start()
 
-    for which in range(2):
-        window_copy(which, 1).wait_send()
-        window_copy(which, 2).wait_send()
-
-        @pl.when(core == 0)
-        def _():
-            window_copy(which, 3).wait_send()
-
-    grad_copy(1).wait_send()
-    grad_copy(2).wait_send()
-
-    @pl.when(core == 1)
-    def _():
-        grad_copy(3).wait_send()
-
-    for by in range(1, head_count):
-        head_copy(down_send, down_recv, down_ss, down_rs, by).wait_send()
-        head_copy(upq_send, upq_recv, upq_ss, upq_rs, by).wait_send()
-        head_copy(upkv_send, upkv_recv, upkv_ss, upkv_rs, by).wait_send()
-    for by in range(1, QUAD):
-        quad_copy(by).wait_send()
-        quad_copy_c(by).wait_send()
-
-    def wait_z(by, _):
-        z_copy(by).wait_send()
-        cz_copy(by, zi).wait_send()
-        for i in range(per_owner):
-            gather_copy(by, zi, i).wait_send()
-        return 0
-
-    lax.fori_loop(1, nz, wait_z, 0)
     for by in range(1, QUAD):
         final_copy(by, quad_at(-by)).wait_recv()
         final_copy_c(by, quad_at(-by)).wait_recv()
         final_copy(by, b).wait_send()
         final_copy_c(by, b).wait_send()
+
+    for wait in pending:
+        wait()
+
+
+def place(
+    kv, x, g, c, down_o, up_q_o, up_kv_o, kv_o, x_o, kv_v, x_v, g_v, c_v, in_sems, out_sems
+):
+    ways = [
+        (x, x_v, [(x_v, x_o)]),
+        (g, g_v, [(g_v.at[: 3 * RANK], down_o), (g_v.at[3 * RANK :], up_q_o)]),
+        (kv, kv_v, [(kv_v, kv_o)]),
+        (c, c_v, [(c_v, up_kv_o)]),
+    ]
+    arriving = [
+        pltpu.make_async_copy(src, dst, in_sems.at[i]) for i, (src, dst, _) in enumerate(ways)
+    ]
+    for copy in arriving:
+        copy.start()
+    leaving = []
+    for copy, (_, _, targets) in zip(arriving, ways):
+        copy.wait()
+        for src, dst in targets:
+            leaving.append(pltpu.make_async_copy(src, dst, out_sems.at[len(leaving)]))
+            leaving[-1].start()
+    for copy in leaving:
+        copy.wait()
 
 
 def per_device(
@@ -453,19 +516,20 @@
     flat_kv_up = key_value_up_weight.reshape(2 * RANK, HEAD_SIZE)
     vmem = pltpu.VMEM
     sem = pltpu.SemaphoreType.DMA
-    anywhere = pl.BlockSpec(memory_space=pl.ANY)
+    anywhere = pl.BlockSpec(memory_space=pltpu.HBM)
     in_vmem = pl.BlockSpec(memory_space=pltpu.VMEM)
-    kv_out, up_out, g_out, c_out = pl.pallas_call(
+    parts = pl.pallas_call(
         functools.partial(kernel, seq_count, head_count),
         out_shape=(
             jax.ShapeDtypeStruct((2, tokens, HEAD_SIZE), BF16),
-            jax.ShapeDtypeStruct((3 * RANK, tokens), BF16),
+            jax.ShapeDtypeStruct((tokens, width), BF16),
             jax.ShapeDtypeStruct((4 * RANK, width), F32),
             jax.ShapeDtypeStruct((2 * RANK, HEAD_SIZE), F32),
         ),
         in_specs=[anywhere] * 5 + [pl.BlockSpec(memory_space=pltpu.SMEM)] + [anywhere] * 4,
         out_specs=(in_vmem,) * 4,
         scratch_shapes=[
+            vmem((3 * RANK, tokens), BF16),
             vmem((tokens, columns), BF16),
             vmem((tokens, columns), BF16),
             vmem((tokens, width), BF16),
@@ -511,24 +575,39 @@
             sem((QUAD,)), sem((QUAD,)),
         ],
         compiler_params=pltpu.CompilerParams(
-            collective_id=0, has_side_effects=True, vmem_limit_bytes=48 * 1024 * 1024
+            collective_id=0, has_side_effects=True, vmem_limit_bytes=VMEM_BYTES
         ),
     )(
         queries, layer_key_rows, layer_value_rows, output_gradient, output_row_sums,
         shifted_head_flags, inputs, flat_down, query_up_weight, flat_kv_up,
     )
-    grad_inputs = (
-        ADAPTER_SCALE
-        * lax.dot_general(
-            up_out, flat_down, (((0,), (0,)), ((), ())), preferred_element_type=F32
-        )
-    ).astype(BF16)
+    down_gradient, grad_up_q, grad_up_kv, kv_gradient, grad_inputs = pl.pallas_call(
+        place,
+        out_shape=(
+            jax.ShapeDtypeStruct((3 * RANK, width), F32),
+            jax.ShapeDtypeStruct((RANK, columns), F32),
+            jax.ShapeDtypeStruct((2 * RANK, HEAD_SIZE), F32),
+            jax.ShapeDtypeStruct((2, tokens, HEAD_SIZE), BF16),
+            jax.ShapeDtypeStruct((tokens, width), BF16),
+        ),
+        in_specs=[anywhere] * 4,
+        out_specs=(anywhere,) * 5,
+        scratch_shapes=[
+            vmem((2, tokens, HEAD_SIZE), BF16),
+            vmem((tokens, width), BF16),
+            vmem((4 * RANK, width), F32),
+            vmem((2 * RANK, HEAD_SIZE), F32),
+            sem((4,)),
+            sem((5,)),
+        ],
+        compiler_params=pltpu.CompilerParams(vmem_limit_bytes=VMEM_BYTES),
+    )(*parts)
     return (
         grad_inputs,
-        kv_out,
-        g_out[: 3 * RANK].reshape(3, RANK, width),
-        g_out[3 * RANK :],
-        c_out.reshape(2, RANK, HEAD_SIZE),
+        kv_gradient,
+        down_gradient.reshape(3, RANK, width),
+        grad_up_q,
+        grad_up_kv.reshape(2, RANK, HEAD_SIZE),
     )
 
 

time: 89.7 us -> 80.2 us (0.89)
  local copies, waits for them, and re-layouts: 11.1 us -> 0 us
  Pallas kernels: 76.3 us -> 79.4 us
  matrix products: 1.11 us -> 0 us
    unnamed x22 -> x0, local copies, waits for them, and re-layouts: 9.75 us -> none
    pallas_call x0 -> x1, Pallas kernels: none -> 2.04 us  [per_device(): pl.pallas_call(place, out_shape=(jax.ShapeDtypeStruct((3 * RANK, width),...]
    slice x2 -> x0, local copies, waits for them, and re-layouts: 1.32 us -> none  [the longest x1 0.69 us: per_device(): g_out[:3 * RANK].reshape(3, RANK, width)]
    dot_general x1 -> x0, matrix products: 1.11 us -> none  [per_device(): lax.dot_general(up_out, flat_down, (((0,), (0,)), ((), ())), preferred_el...]
    pallas_call x1, Pallas kernels: 76.3 us -> 77.3 us  [per_device(): pl.pallas_call(functools.partial(kernel, seq_count, head_count), out_shap...]
where the time goes in v2:
time: 80.2 us; the launch traced here: 80 us
  Pallas kernels  79.4 us (99%)
    pallas_call x1, Pallas kernels, per_device(): pl.pallas_call(functools.partial(kernel, seq_count, head_count), out_shap...  77.3 us
    pallas_call x1, Pallas kernels, per_device(): pl.pallas_call(place, out_shape=(jax.ShapeDtypeStruct((3 * RANK, width),...  2.04 us

profile of v2, /device:TPU:1, one launch (start us, length us, event | category | flops | bytes accessed | tf_op | source)
XLA Modules:
  0.0 80.0 jit_solution(7143922584207619056)
XLA Ops:
  0.6 77.3 %shard_map.137 = (bf16[2,256,128]{2,1,0:T(8,128)(2,1)}, bf16[256,1024]{1,0:T(8,128)(2,1)}, f32[64,1024]{1,0:T(8,128)}, f32[32,128]{1,0:T(8,128)}) custom-call(bf16[256,1024]{1,0:T(8,128)(2,1)} %q_hbm.1, bf16[256,128]{1,0:T(8,128)(2,1)} %k_hbm.1, bf16[256,128]{1,0:T(8,128)(2,1)} %v_hbm.1, bf16[256,1024]{1,0:T(8,128)(2,1)} %do_hbm.1, f32[8,256]{1,0:T(8,128)} %rs_hbm.1, ...), custom_call_target="tpu_custom_call" | custom-call | tf_op jit(solution)/shard_map/pallas_call | solution.py:521
  78.0 2.0 %shard_map.138 = (f32[48,1024]{1,0:T(8,128)}, f32[16,1024]{1,0:T(8,128)}, f32[32,128]{1,0:T(8,128)}, bf16[2,256,128]{2,1,0:T(8,128)(2,1)}, bf16[256,1024]{1,0:T(8,128)(2,1)}) custom-call(bf16[2,256,128]{2,1,0:T(8,128)(2,1)} %get-tuple-element.14.kv, bf16[256,1024]{1,0:T(8,128)(2,1)} %get-tuple-element.15.x, f32[64,1024]{1,0:T(8,128)} %get-tuple-element.16.g, ...), custom_call_target="tpu_custom_call" | custom-call | tf_op jit(solution)/shard_map/pallas_call | solution.py:584

commit v3 on v2

v3 whole, which is shorter than its diff:
```python
import functools
import math

import jax
import jax.numpy as jnp
from jax import lax
from jax.experimental import pallas as pl
from jax.experimental.pallas import tpu as pltpu
from jax.sharding import PartitionSpec as P

HEAD_SIZE = 128
GROUP = 1024
RANK = 16
QUAD = 4
UNITS = 16
LOG2E = 1.4426950408889634
BIG = 1e30
ADAPTER_SCALE = 2.0
VMEM_BYTES = 63 * 1024 * 1024

MESH = pl.DeviceIdType.MESH
F32 = jnp.float32
BF16 = jnp.bfloat16


def dot_nn(a, b):
    return lax.dot_general(a, b, (((1,), (0,)), ((), ())), preferred_element_type=F32)


def dot_nt(a, b):
    return lax.dot_general(a, b, (((1,), (1,)), ((), ())), preferred_element_type=F32)


def kernel(
    seq_count,
    head_count,
    q_hbm, k_hbm, v_hbm, do_hbm, rs_hbm, flags, x_hbm, wd_hbm, wq_hbm, wkv_hbm,
    kv_out, x_out, g_out, c_out,
    up_out, q_v, do_v, x_v, wd_v, wq_v, wkv_v, rs_v,
    kwin, vwin, k_t, scores, tops, probs, dscores, own_kv, kv_send, kv_recv, relay,
    down_send, down_recv, down_low, upq_send, upq_recv, upkv_send, upkv_recv,
    g_full, g_pair, c_full, c_pair, units, slots, c_sum, c_slots,
    load_sem, win_ss, win_rs, down_ss, down_rs, upq_ss, upq_rs, upkv_ss, upkv_rs,
    relay_ss, relay_rs, kv_ss, kv_rs, pair_ss, pair_rs, rs_ss, rs_rs, c_ss, c_rs,
    ag_ss, ag_rs, cag_ss, cag_rs, fin_ss, fin_rs, known,
):
    tokens = q_v.shape[0]
    heads = q_v.shape[1] // HEAD_SIZE
    nz = seq_count // QUAD
    per_owner = UNITS // nz
    half = x_v.shape[1] // 2
    s = lax.axis_index("seq")
    hd = lax.axis_index("head")
    zi = s // QUAD
    core = s % 2
    x_lo = (s % QUAD) // 2
    sibling = s + 1 - 2 * core
    scale = HEAD_SIZE ** -0.5
    multiplier = ADAPTER_SCALE / math.sqrt(tokens * seq_count)
    pending = []

    def seq_at(by):
        return lax.rem(s + by + seq_count, seq_count)

    def head_at(by):
        return lax.rem(hd + by + head_count, head_count)

    def z_at(by):
        return lax.rem(zi + by + nz, nz)

    def chip(by, x):
        return z_at(by) * QUAD + x * 2 + core

    def remote(src, dst, ss, rs, target):
        return pltpu.make_async_remote_copy(
            src_ref=src, dst_ref=dst, send_sem=ss, recv_sem=rs,
            device_id={"seq": target}, device_id_type=MESH,
        )

    loads = [
        pltpu.make_async_copy(src, dst, load_sem.at[i])
        for i, (src, dst) in enumerate([
            (k_hbm, kwin.at[3]), (q_hbm, q_v), (x_hbm, x_v), (wd_hbm, wd_v), (v_hbm, vwin.at[3]),
            (do_hbm, do_v), (rs_hbm, rs_v), (wq_hbm, wq_v), (wkv_hbm, wkv_v),
        ])
    ]
    for copy in loads:
        copy.start()

    barrier = pltpu.get_barrier_semaphore()
    near = [sibling, seq_at(2), seq_at(-2), seq_at(4), seq_at(-4)]
    for target in near:
        pl.semaphore_signal(barrier, inc=1, device_id={"seq": target}, device_id_type=MESH)
    for by in range(1, head_count):
        pl.semaphore_signal(barrier, inc=1, device_id={"head": head_at(by)}, device_id_type=MESH)
    pl.semaphore_wait(barrier, len(near) + head_count - 1)

    rounds = []
    step = 2
    while step < nz:
        rounds.append(step)
        step *= 2

    def tell(i):
        if i < len(rounds):
            for by in (2 * rounds[i], -2 * rounds[i]):
                pl.semaphore_signal(
                    known.at[i], inc=1, device_id={"seq": seq_at(by)}, device_id_type=MESH
                )

    def hear(i):
        if i < len(rounds):
            pl.semaphore_wait(known.at[i], 2)

    own = (k_hbm, v_hbm)
    win = (kwin, vwin)

    def cross(c):
        return remote(own[c], win[c].at[1], win_ss.at[c, 0], win_rs.at[c, 1], seq_at(2))

    def give(c):
        return remote(own[c], win[c].at[2], win_ss.at[c, 1], win_rs.at[c, 2], sibling)

    def forward(c, slot):
        return remote(win[c].at[1], win[c].at[slot], win_ss.at[c, 2], win_rs.at[c, slot], sibling)

    for c in range(2):
        cross(c).start()

        @pl.when(core == 0)
        def _():
            give(c).start()

    tell(0)

    def head_copy(src, dst, ss, rs, by):
        return pltpu.make_async_remote_copy(
            src_ref=src, dst_ref=dst.at[by], send_sem=ss.at[by], recv_sem=rs.at[by],
            device_id={"head": head_at(by)}, device_id_type=MESH,
        )

    def head_start(*args):
        for by in range(1, head_count):
            head_copy(*args, by).start()

        def wait():
            for by in range(1, head_count):
                head_copy(*args, by).wait_send()

        pending.append(wait)

    row_id = lax.broadcasted_iota(jnp.int32, (tokens, tokens), 0)
    col_id = lax.broadcasted_iota(jnp.int32, (tokens, tokens), 1)
    causal = jnp.where(row_id <= col_id, 0.0, -BIG).astype(F32)
    want = (1 - x_lo).astype(F32)
    even = (1 - core).astype(F32)
    c2 = scale * LOG2E

    def head_cols(ref, h):
        return ref[:, pl.ds(pl.multiple_of(h * HEAD_SIZE, HEAD_SIZE), HEAD_SIZE)]

    def rows(j):
        return pl.ds(j * tokens, tokens)

    def over_heads(body, at_once=2):
        def some(i, _):
            for k in range(at_once):
                body(i * at_once + k)
            return 0

        lax.fori_loop(0, heads // at_once, some, 0)

    def score_block(j):
        def one(h):
            score = dot_nt(kwin[j], head_cols(q_v, h))
            if j == 3:
                score = score + causal
            scores[h, rows(j), :] = score
            tops[j, pl.ds(h, 1), :] = jnp.max(score, axis=0, keepdims=True)

        over_heads(one)
        k_t[:, j * tokens : (j + 1) * tokens] = kwin[j].astype(F32).T.astype(BF16)

    loads[0].wait()
    loads[1].wait()
    score_block(3)
    loads[2].wait()
    loads[3].wait()
    down_part = dot_nt(wd_v[...], x_v[...])
    down_send[...] = down_part.astype(BF16)
    hear(0)
    tell(1)

    def rest_of_scores(odd):
        if odd:
            give(0).wait_recv()
            score_block(2)
            cross(0).wait_recv()
            forward(0, 2).start()
            score_block(1)
            forward(0, 0).wait_recv()
            score_block(0)
        else:
            cross(0).wait_recv()
            forward(0, 0).start()
            score_block(1)
            forward(0, 2).wait_recv()
            score_block(2)

    def pass_values_on(odd):
        cross(1).wait_recv()
        forward(1, 2 if odd else 0).start()

    def relay_copy(slot):
        return remote(kv_send.at[slot], relay, relay_ss, relay_rs, sibling)

    def back_copy():
        return remote(kv_send.at[1], kv_recv.at[0], kv_ss.at[0], kv_rs.at[0], seq_at(-2))

    def home_copy():
        return remote(kv_send.at[2], kv_recv.at[1], kv_ss.at[1], kv_rs.at[1], sibling)

    def attention(odd):
        order = (0, 1, 2, 3) if odd else (2, 1, 3)

        def weights(h):
            differs = flags[h].astype(F32) - want
            far = differs * differs * BIG
            bias = {0: far, 1: far, 2: 0.0 if odd else far, 3: 0.0}
            at = pl.ds(h, 1)
            top = None
            for j in order:
                high = tops[j, at, :] - bias[j]
                top = high if top is None else jnp.maximum(top, high)
            weight = {}
            total = None
            for j in order:
                weight[j] = jnp.exp2(scores[h, rows(j), :] * c2 - (top * c2 + bias[j]))
                part = jnp.sum(weight[j], axis=0, keepdims=True)
                total = part if total is None else total + part
            inverse = 1.0 / total
            for j in order:
                probs[h, rows(j), :] = (weight[j] * inverse).astype(BF16)

        over_heads(weights, 1)

        if odd:
            give(1).wait_recv()
            forward(1, 0).wait_recv()
        else:
            forward(1, 2).wait_recv()
        for j in order:

            def backward(i, acc):
                dk, dv = acc
                for k in range(2):
                    h = i * 2 + k
                    q = head_cols(q_v, h)
                    do = head_cols(do_v, h)
                    p = probs[h, rows(j), :]
                    dp = dot_nt(vwin[j], do)
                    ds = (p.astype(F32) * (dp - rs_v[pl.ds(h, 1), :])).astype(BF16)
                    dscores[h, rows(j), :] = ds
                    dk = dk + dot_nn(ds, q)
                    dv = dv + dot_nn(p, do)
                return dk, dv

            zero = jnp.zeros((tokens, HEAD_SIZE), F32)
            dk, dv = lax.fori_loop(0, heads // 2, backward, (zero, zero))
            dk = dk * scale
            if j == 3:
                own_kv[0] = dk
                own_kv[1] = dv
            elif j == 1:
                relay_copy(2).wait_recv()
                kv_send[1, 0] = (dk + relay[0].astype(F32)).astype(BF16)
                kv_send[1, 1] = (dv + relay[1].astype(F32)).astype(BF16)
                back_copy().start()
            else:
                kv_send[j, 0] = dk.astype(BF16)
                kv_send[j, 1] = dv.astype(BF16)
                if j == 0 or not odd:
                    relay_copy(j).start()
                else:
                    home_copy().start()

    def split(fn):
        @pl.when(core == 1)
        def _():
            fn(True)

        @pl.when(core == 0)
        def _():
            fn(False)

    split(rest_of_scores)
    head_start(down_send, down_recv, down_ss, down_rs)
    hear(1)
    tell(2)
    for i in range(4, 9):
        loads[i].wait()
    split(pass_values_on)

    def window_sent(odd):
        for c in range(2):
            cross(c).wait_send()
            forward(c, 2 if odd else 0).wait_send()
            if not odd:
                give(c).wait_send()

    pending.append(lambda: split(window_sent))
    split(attention)

    def grads_sent(odd):
        relay_copy(0 if odd else 2).wait_send()
        back_copy().wait_send()
        if odd:
            home_copy().wait_send()

    pending.append(lambda: split(grads_sent))

    down = down_part
    for by in range(1, head_count):
        head_copy(down_send, down_recv, down_ss, down_rs, by).wait_recv()
        down = down + down_recv[by].astype(F32)
    down_low[...] = down.astype(BF16)

    def query_grads(odd):
        first = 0 if odd else tokens
        per_half = heads // 2

        def one(i, acc):
            for k in range(2):
                h = i * 2 + k
                dq = (dot_nn(k_t[:, first:], dscores[h, first:, :]) * scale).astype(BF16)
                cols = pl.ds(pl.multiple_of((h % per_half) * HEAD_SIZE, HEAD_SIZE), HEAD_SIZE)
                g_full[h // per_half, :RANK, cols] = dot_nt(down_low[:RANK, :], dq)
                acc = acc + dot_nn(head_cols(wq_v, h), dq)
            return acc

        acc = lax.fori_loop(0, heads // 2, one, jnp.zeros((RANK, tokens), F32))
        upq_send[...] = acc.astype(BF16)

    split(query_grads)
    head_start(upq_send, upq_recv, upq_ss, upq_rs)
    hear(2)

    back_copy().wait_recv()

    @pl.when(core == 0)
    def _():
        home_copy().wait_recv()
        own_kv[...] = own_kv[...] + kv_recv[1].astype(F32)

    dkv = (own_kv[...] + kv_recv[0].astype(F32)).astype(BF16)
    kv_out[...] = dkv
    for c in range(2):
        upkv_send[c * RANK : (c + 1) * RANK, :] = dot_nt(
            wkv_v[c * RANK : (c + 1) * RANK, :], dkv[c]
        ).astype(BF16)
    head_start(upkv_send, upkv_recv, upkv_ss, upkv_rs)
    for c in range(2):
        c_full[c] = dot_nn(down_low[(c + 1) * RANK : (c + 2) * RANK, :], dkv[c])

    part_rows = 2 * RANK

    def pair_copy(p):
        at = pl.ds(p * part_rows, part_rows)
        return remote(
            g_full.at[1 - core, at], g_pair.at[at], pair_ss.at[p], pair_rs.at[p], sibling
        )

    def pair_copy_c():
        return remote(c_full.at[1 - core], c_pair, pair_ss.at[2], pair_rs.at[2], sibling)

    pair_copy_c().start()
    pending.append(lambda: pair_copy_c().wait_send())

    def head_total(send, recv, ss, rs):
        total = send[...].astype(F32)
        for by in range(1, head_count):
            head_copy(send, recv, ss, rs, by).wait_recv()
            total = total + recv[by].astype(F32)
        return total.astype(BF16)

    def down_rows(first, last):
        for c in range(2):
            g_full[c, RANK + first : RANK + last, :] = dot_nn(
                up_out[first:last, :], x_v[:, c * half : (c + 1) * half]
            )

    def far_first(i):
        return nz // 2 + lax.rem(i + 1, 2) * (i // 2) - lax.rem(i, 2) * ((i + 1) // 2)

    def scatter_copy(p, by, x):
        slot = x * nz + by
        return remote(
            units.at[p, z_at(by)], slots.at[slot], rs_ss.at[p, by], rs_rs.at[slot], chip(by, p)
        )

    def loop(first, last, fn):
        def body(i, _):
            fn(i)
            return 0

        lax.fori_loop(first, last, body, 0)

    def at_x(p, fn):
        @pl.when(x_lo == p)
        def _():
            fn(nz - 1)

        @pl.when(x_lo != p)
        def _():
            fn(nz)

    def scatter(p):
        pair_copy(p).wait_recv()
        at = pl.ds(p * part_rows, part_rows)
        g = g_full[core, at, :] + g_pair[at, :]
        for u in range(UNITS):
            r, col = (u // 4) * 8, (u % 4) * 128
            units[p, u // per_owner, u % per_owner] = g[r : r + 8, col : col + 128]
        at_x(p, lambda n: loop(0, n, lambda i: scatter_copy(p, far_first(i), x_lo).start()))
        pending.append(
            lambda: at_x(
                p, lambda n: loop(0, n, lambda i: scatter_copy(p, far_first(i), x_lo).wait_send())
            )
        )

    up_out[:RANK, :] = head_total(upq_send, upq_recv, upq_ss, upq_rs)
    down_rows(0, RANK)
    pair_copy(0).start()
    pending.append(lambda: pair_copy(0).wait_send())
    scatter(0)

    c_owner = (nz // 2) * QUAD + 2 + core
    is_c_owner = s == c_owner

    def c_copy(slot):
        return remote(c_sum, c_slots.at[slot], c_ss, c_rs.at[slot], c_owner)

    pair_copy_c().wait_recv()
    c_sum[...] = c_full[core] + c_pair[...]

    @pl.when(jnp.logical_not(is_c_owner))
    def _():
        c_copy(x_lo * nz + zi).start()

    def c_sent():
        @pl.when(jnp.logical_not(is_c_owner))
        def _():
            c_copy(x_lo * nz + zi).wait_send()

    pending.append(c_sent)

    up_out[RANK:, :] = head_total(upkv_send, upkv_recv, upkv_ss, upkv_rs)
    down_rows(RANK, 3 * RANK)
    pair_copy(1).start()
    pending.append(lambda: pair_copy(1).wait_send())
    scatter(1)

    for c in range(4):
        cols = slice(c * half // 2, (c + 1) * half // 2)
        part = lax.dot_general(
            up_out[...], wd_v[:, cols], (((0,), (0,)), ((), ())), preferred_element_type=F32
        )
        x_out[:, cols] = (ADAPTER_SCALE * part).astype(BF16)

    def unit_ref(p, u):
        return g_out.at[
            pl.ds(pl.multiple_of(p * part_rows + (u // 4) * 8, 8), 8),
            pl.ds(pl.multiple_of(core * half + (u % 4) * 128, 128), 128),
        ]

    def gather_copy(p, owner, i, by, x):
        u = owner * per_owner + i
        ref = unit_ref(p, u)
        return remote(
            ref, ref, ag_ss.at[(x * nz + by) * per_owner + i], ag_rs.at[p, u], chip(by, x)
        )

    def each_target(p, fn):
        loop(0, nz - 1, lambda i: (fn(far_first(i), 0), fn(far_first(i), 1)))
        fn(0, 1 - p)

    def gather(p):
        @pl.when(x_lo == p)
        def _():
            total = units[p, zi]
            for by in range(0, nz):
                for x in (p, 1 - p):
                    if by == 0 and x == p:
                        continue
                    scatter_copy(p, by, x).wait_recv()
                    total = total + slots[x * nz + by]
            total = total * multiplier
            for i in range(per_owner):
                unit_ref(p, zi * per_owner + i)[...] = total[i]

            def start(by, x):
                for i in range(per_owner):
                    gather_copy(p, zi, i, by, x).start()

            each_target(p, start)

    def gather_sent():
        for p in range(2):

            @pl.when(x_lo == p)
            def _():
                def wait(by, x):
                    for i in range(per_owner):
                        gather_copy(p, zi, i, by, x).wait_send()

                each_target(p, wait)

    def c_ref():
        return c_out.at[pl.ds(pl.multiple_of(core * RANK, RANK), RANK), :]

    def c_gather_copy(by, x):
        return remote(c_ref(), c_ref(), cag_ss.at[x * nz + by], cag_rs, chip(by, x))

    gather(0)

    @pl.when(is_c_owner)
    def _():
        total = c_sum[...]
        for by in range(0, nz):
            for x in (1, 0):
                if by == 0 and x == 1:
                    continue
                slot = x * nz + z_at(by)
                c_copy(slot).wait_recv()
                total = total + c_slots[slot]
        c_out[pl.ds(pl.multiple_of(core * RANK, RANK), RANK), :] = total * multiplier
        each_target(1, lambda by, x: c_gather_copy(by, x).start())

    def c_gather_sent():
        @pl.when(is_c_owner)
        def _():
            each_target(1, lambda by, x: c_gather_copy(by, x).wait_send())

    gather(1)
    pending.append(gather_sent)
    pending.append(c_gather_sent)

    def wait_gathered(p):
        def wait(by):
            for i in range(per_owner):
                gather_copy(p, z_at(by), i, by, 0).wait_recv()

        loop(1, nz, wait)

        @pl.when(x_lo != p)
        def _():
            wait(0)

    def final_copy(p, side):
        ref = g_out.at[
            pl.ds(p * part_rows, part_rows), pl.ds(pl.multiple_of(side * half, 128), half)
        ]
        return remote(ref, ref, fin_ss.at[p], fin_rs.at[p], sibling)

    def final_copy_c(side):
        ref = c_out.at[pl.ds(pl.multiple_of(side * RANK, RANK), RANK), :]
        return remote(ref, ref, fin_ss.at[2], fin_rs.at[2], sibling)

    wait_gathered(0)
    final_copy(0, core).start()

    @pl.when(jnp.logical_not(is_c_owner))
    def _():
        c_gather_copy(0, 0).wait_recv()

    final_copy_c(core).start()
    wait_gathered(1)
    final_copy(1, core).start()

    for wait in pending:
        wait()
    final_copy_c(1 - core).wait_recv()
    final_copy_c(core).wait_send()
    for p in range(2):
        final_copy(p, 1 - core).wait_recv()
        final_copy(p, core).wait_send()


def place(
    kv, x, g, c, down_o, up_q_o, up_kv_o, kv_o, x_o, kv_v, x_v, g_v, c_v, in_sems, out_sems
):
    ways = [
        (x, x_v, [(x_v, x_o)]),
        (g, g_v, [(g_v.at[RANK:], down_o), (g_v.at[:RANK], up_q_o)]),
        (kv, kv_v, [(kv_v, kv_o)]),
        (c, c_v, [(c_v, up_kv_o)]),
    ]
    arriving = [
        pltpu.make_async_copy(src, dst, in_sems.at[i]) for i, (src, dst, _) in enumerate(ways)
    ]
    for copy in arriving:
        copy.start()
    leaving = []
    for copy, (_, _, targets) in zip(arriving, ways):
        copy.wait()
        for src, dst in targets:
            leaving.append(pltpu.make_async_copy(src, dst, out_sems.at[len(leaving)]))
            leaving[-1].start()
    for copy in leaving:
        copy.wait()


def per_device(
    queries, layer_key_rows, layer_value_rows, output_gradient, output_row_sums,
    shifted_head_flags, inputs, adapter_down_weight, query_up_weight, key_value_up_weight,
):
    seq_count = lax.axis_size("seq")
    head_count = lax.axis_size("head")
    tokens, columns = queries.shape
    heads = columns // HEAD_SIZE
    width = inputs.shape[1]
    nz = seq_count // QUAD
    per_owner = UNITS // nz
    flat_down = adapter_down_weight.reshape(3 * RANK, width)
    flat_kv_up = key_value_up_weight.reshape(2 * RANK, HEAD_SIZE)
    vmem = pltpu.VMEM
    sem = pltpu.SemaphoreType.DMA
    anywhere = pl.BlockSpec(memory_space=pltpu.HBM)
    in_vmem = pl.BlockSpec(memory_space=pltpu.VMEM)
    parts = pl.pallas_call(
        functools.partial(kernel, seq_count, head_count),
        out_shape=(
            jax.ShapeDtypeStruct((2, tokens, HEAD_SIZE), BF16),
            jax.ShapeDtypeStruct((tokens, width), BF16),
            jax.ShapeDtypeStruct((4 * RANK, width), F32),
            jax.ShapeDtypeStruct((2 * RANK, HEAD_SIZE), F32),
        ),
        in_specs=[anywhere] * 5 + [pl.BlockSpec(memory_space=pltpu.SMEM)] + [anywhere] * 4,
        out_specs=(in_vmem,) * 4,
        scratch_shapes=[
            vmem((3 * RANK, tokens), BF16),
            vmem((tokens, columns), BF16),
            vmem((tokens, columns), BF16),
            vmem((tokens, width), BF16),
            vmem((3 * RANK, width), BF16),
            vmem((RANK, columns), BF16),
            vmem((2 * RANK, HEAD_SIZE), BF16),
            vmem((heads, tokens), F32),
            vmem((4, tokens, HEAD_SIZE), BF16),
            vmem((4, tokens, HEAD_SIZE), BF16),
            vmem((HEAD_SIZE, 4 * tokens), BF16),
            vmem((heads, 4 * tokens, tokens), F32),
            vmem((4, heads, tokens), F32),
            vmem((heads, 4 * tokens, tokens), BF16),
            vmem((heads, 4 * tokens, tokens), BF16),
            vmem((2, tokens, HEAD_SIZE), F32),
            vmem((3, 2, tokens, HEAD_SIZE), BF16),
            vmem((2, 2, tokens, HEAD_SIZE), BF16),
            vmem((2, tokens, HEAD_SIZE), BF16),
            vmem((3 * RANK, tokens), BF16),
            vmem((head_count, 3 * RANK, tokens), BF16),
            vmem((3 * RANK, tokens), BF16),
            vmem((RANK, tokens), BF16),
            vmem((head_count, RANK, tokens), BF16),
            vmem((2 * RANK, tokens), BF16),
            vmem((head_count, 2 * RANK, tokens), BF16),
            vmem((2, 4 * RANK, width // 2), F32),
            vmem((4 * RANK, width // 2), F32),
            vmem((2, RANK, HEAD_SIZE), F32),
            vmem((RANK, HEAD_SIZE), F32),
            vmem((2, nz, per_owner, 8, 128), F32),
            vmem((2 * nz, per_owner, 8, 128), F32),
            vmem((RANK, HEAD_SIZE), F32),
            vmem((2 * nz, RANK, HEAD_SIZE), F32),
            sem((9,)),
            sem((2, 3)), sem((2, 4)),
            sem((head_count,)), sem((head_count,)),
            sem((head_count,)), sem((head_count,)),
            sem((head_count,)), sem((head_count,)),
            sem, sem,
            sem((2,)), sem((2,)),
            sem((3,)), sem((3,)),
            sem((2, nz)), sem((2 * nz,)),
            sem, sem((2 * nz,)),
            sem((2 * nz * per_owner,)), sem((2, UNITS)),
            sem((2 * nz,)), sem,
            sem((3,)), sem((3,)),
            pltpu.SemaphoreType.REGULAR((3,)),
        ],
        compiler_params=pltpu.CompilerParams(
            collective_id=0, has_side_effects=True, vmem_limit_bytes=VMEM_BYTES
        ),
    )(
        queries, layer_key_rows, layer_value_rows, output_gradient, output_row_sums,
        shifted_head_flags, inputs, flat_down, query_up_weight, flat_kv_up,
    )
    down_gradient, grad_up_q, grad_up_kv, kv_gradient, grad_inputs = pl.pallas_call(
        place,
        out_shape=(
            jax.ShapeDtypeStruct((3 * RANK, width), F32),
            jax.ShapeDtypeStruct((RANK, columns), F32),
            jax.ShapeDtypeStruct((2 * RANK, HEAD_SIZE), F32),
            jax.ShapeDtypeStruct((2, tokens, HEAD_SIZE), BF16),
            jax.ShapeDtypeStruct((tokens, width), BF16),
        ),
        in_specs=[anywhere] * 4,
        out_specs=(anywhere,) * 5,
        scratch_shapes=[
            vmem((2, tokens, HEAD_SIZE), BF16),
            vmem((tokens, width), BF16),
            vmem((4 * RANK, width), F32),
            vmem((2 * RANK, HEAD_SIZE), F32),
            sem((4,)),
            sem((5,)),
        ],
        compiler_params=pltpu.CompilerParams(vmem_limit_bytes=VMEM_BYTES),
    )(*parts)
    return (
        grad_inputs,
        kv_gradient,
        down_gradient.reshape(3, RANK, width),
        grad_up_q,
        grad_up_kv.reshape(2, RANK, HEAD_SIZE),
    )


def solution(mesh):
    placed = (
        P("seq", "head"),
        P("seq", "head"),
        P("seq", "head"),
        P("seq", "head"),
        P("head", "seq"),
        P("head"),
        P("seq", "head"),
        P(None, None, "head"),
        P(None, "head"),
        P(None, None, "head"),
    )
    return jax.shard_map(
        per_device,
        mesh=mesh,
        in_specs=placed,
        out_specs=(
            P("seq", "head"),
            P(None, "seq", "head"),
            P(None, None, "head"),
            P(None, "head"),
            P(None, None, "head"),
        ),
        check_vma=False,
    )
```

time: 80.2 us -> 70.5 us (0.88)
  Pallas kernels: 79.4 us -> 69.7 us
    pallas_call x1, Pallas kernels: 77.3 us -> 67.7 us  [per_device(): pl.pallas_call(functools.partial(kernel, seq_count, head_count), out_shap...]
where the time goes in v3:
time: 70.5 us; the launch traced here: 70.4 us
  Pallas kernels  69.7 us (99%)
    pallas_call x1, Pallas kernels, per_device(): pl.pallas_call(functools.partial(kernel, seq_count, head_count), out_shap...  67.7 us
    pallas_call x1, Pallas kernels, per_device(): pl.pallas_call(place, out_shape=(jax.ShapeDtypeStruct((3 * RANK, width),...  2.04 us

profile of v3, /device:TPU:1, one launch (start us, length us, event | category | flops | bytes accessed | tf_op | source)
XLA Modules:
  0.0 70.4 jit_solution(11257230066931548708)
XLA Ops:
  0.6 67.7 %shard_map.137 = (bf16[2,256,128]{2,1,0:T(8,128)(2,1)}, bf16[256,1024]{1,0:T(8,128)(2,1)}, f32[64,1024]{1,0:T(8,128)}, f32[32,128]{1,0:T(8,128)}) custom-call(bf16[256,1024]{1,0:T(8,128)(2,1)} %q_hbm.1, bf16[256,128]{1,0:T(8,128)(2,1)} %k_hbm.1, bf16[256,128]{1,0:T(8,128)(2,1)} %v_hbm.1, bf16[256,1024]{1,0:T(8,128)(2,1)} %do_hbm.1, f32[8,256]{1,0:T(8,128)} %rs_hbm.1, ...), custom_call_target="tpu_custom_call" | custom-call | tf_op jit(solution)/shard_map/pallas_call | solution.py:630
  68.3 2.0 %shard_map.138 = (f32[48,1024]{1,0:T(8,128)}, f32[16,1024]{1,0:T(8,128)}, f32[32,128]{1,0:T(8,128)}, bf16[2,256,128]{2,1,0:T(8,128)(2,1)}, bf16[256,1024]{1,0:T(8,128)(2,1)}) custom-call(bf16[2,256,128]{2,1,0:T(8,128)(2,1)} %get-tuple-element.14.kv, bf16[256,1024]{1,0:T(8,128)(2,1)} %get-tuple-element.15.x, f32[64,1024]{1,0:T(8,128)} %get-tuple-element.16.g, ...), custom_call_target="tpu_custom_call" | custom-call | tf_op jit(solution)/shard_map/pallas_call | solution.py:697

commit v4 on v3

--- a/solution.py
+++ b/solution.py
@@ -34,13 +34,13 @@
 def kernel(
     seq_count,
     head_count,
-    q_hbm, k_hbm, v_hbm, do_hbm, rs_hbm, flags, x_hbm, wd_hbm, wq_hbm, wkv_hbm,
-    kv_out, x_out, g_out, c_out,
-    up_out, q_v, do_v, x_v, wd_v, wq_v, wkv_v, rs_v,
+    q_hbm, k_hbm, v_hbm, do_hbm, rs_hbm, flags_hbm, x_hbm, wd_hbm, wq_hbm, wkv_hbm,
+    kv_hbm, xo_hbm, g_hbm, c_hbm,
+    kv_out, x_out, g_out, c_out, up_out, q_v, do_v, x_v, wd_v, wq_v, wkv_v, rs_v,
     kwin, vwin, k_t, scores, tops, probs, dscores, own_kv, kv_send, kv_recv, relay,
-    down_send, down_recv, down_low, upq_send, upq_recv, upkv_send, upkv_recv,
+    flags, down_send, down_recv, down_low, upq_send, upq_recv, upkv_send, upkv_recv,
     g_full, g_pair, c_full, c_pair, units, slots, c_sum, c_slots,
-    load_sem, win_ss, win_rs, down_ss, down_rs, upq_ss, upq_rs, upkv_ss, upkv_rs,
+    load_sem, out_sem, win_ss, win_rs, down_ss, down_rs, upq_ss, upq_rs, upkv_ss, upkv_rs,
     relay_ss, relay_rs, kv_ss, kv_rs, pair_ss, pair_rs, rs_ss, rs_rs, c_ss, c_rs,
     ag_ss, ag_rs, cag_ss, cag_rs, fin_ss, fin_rs, known,
 ):
@@ -81,7 +81,7 @@
         pltpu.make_async_copy(src, dst, load_sem.at[i])
         for i, (src, dst) in enumerate([
             (k_hbm, kwin.at[3]), (q_hbm, q_v), (x_hbm, x_v), (wd_hbm, wd_v), (v_hbm, vwin.at[3]),
-            (do_hbm, do_v), (rs_hbm, rs_v), (wq_hbm, wq_v), (wkv_hbm, wkv_v),
+            (do_hbm, do_v), (rs_hbm, rs_v), (wq_hbm, wq_v), (wkv_hbm, wkv_v), (flags_hbm, flags),
         ])
     ]
     for copy in loads:
@@ -157,28 +157,18 @@
     c2 = scale * LOG2E
 
     def head_cols(ref, h):
-        return ref[:, pl.ds(pl.multiple_of(h * HEAD_SIZE, HEAD_SIZE), HEAD_SIZE)]
+        return ref[:, h * HEAD_SIZE : (h + 1) * HEAD_SIZE]
 
     def rows(j):
         return pl.ds(j * tokens, tokens)
 
-    def over_heads(body, at_once=2):
-        def some(i, _):
-            for k in range(at_once):
-                body(i * at_once + k)
-            return 0
-
-        lax.fori_loop(0, heads // at_once, some, 0)
-
     def score_block(j):
-        def one(h):
+        for h in range(heads):
             score = dot_nt(kwin[j], head_cols(q_v, h))
             if j == 3:
                 score = score + causal
             scores[h, rows(j), :] = score
-            tops[j, pl.ds(h, 1), :] = jnp.max(score, axis=0, keepdims=True)
-
-        over_heads(one)
+            tops[j, h : h + 1, :] = jnp.max(score, axis=0, keepdims=True)
         k_t[:, j * tokens : (j + 1) * tokens] = kwin[j].astype(F32).T.astype(BF16)
 
     loads[0].wait()
@@ -211,19 +201,23 @@
         cross(1).wait_recv()
         forward(1, 2 if odd else 0).start()
 
-    def relay_copy(slot):
-        return remote(kv_send.at[slot], relay, relay_ss, relay_rs, sibling)
-
-    def back_copy():
-        return remote(kv_send.at[1], kv_recv.at[0], kv_ss.at[0], kv_rs.at[0], seq_at(-2))
+    def relay_copy(slot, c):
+        return remote(
+            kv_send.at[slot, c], relay.at[c], relay_ss.at[c], relay_rs.at[c], sibling
+        )
+
+    def back_copy(c):
+        return remote(
+            kv_send.at[1, c], kv_recv.at[0, c], kv_ss.at[c], kv_rs.at[c], seq_at(-2)
+        )
 
     def home_copy():
-        return remote(kv_send.at[2], kv_recv.at[1], kv_ss.at[1], kv_rs.at[1], sibling)
+        return remote(kv_send.at[2], kv_recv.at[1], kv_ss.at[2], kv_rs.at[2], sibling)
 
     def attention(odd):
         order = (0, 1, 2, 3) if odd else (2, 1, 3)
 
-        def weights(h):
+        def weights(h, _):
             differs = flags[h].astype(F32) - want
             far = differs * differs * BIG
             bias = {0: far, 1: far, 2: 0.0 if odd else far, 3: 0.0}
@@ -241,48 +235,42 @@
             inverse = 1.0 / total
             for j in order:
                 probs[h, rows(j), :] = (weight[j] * inverse).astype(BF16)
-
-        over_heads(weights, 1)
-
+            return 0
+
+        lax.fori_loop(0, heads, weights, 0)
+
+    def summed(left, right, j):
+        total = None
+        for h in range(heads):
+            part = dot_nn(left[h, rows(j), :], head_cols(right, h))
+            total = part if total is None else total + part
+        return total
+
+    def value_grad(j):
+        return summed(probs, do_v, j)
+
+    def key_grad(j):
+        for h in range(heads):
+            p = probs[h, rows(j), :].astype(F32)
+            dp = dot_nt(vwin[j], head_cols(do_v, h))
+            dscores[h, rows(j), :] = (p * (dp - rs_v[h : h + 1, :])).astype(BF16)
+        return summed(dscores, q_v, j) * scale
+
+    def relayed(odd):
+        slot = 0 if odd else 2
         if odd:
-            give(1).wait_recv()
             forward(1, 0).wait_recv()
         else:
             forward(1, 2).wait_recv()
-        for j in order:
-
-            def backward(i, acc):
-                dk, dv = acc
-                for k in range(2):
-                    h = i * 2 + k
-                    q = head_cols(q_v, h)
-                    do = head_cols(do_v, h)
-                    p = probs[h, rows(j), :]
-                    dp = dot_nt(vwin[j], do)
-                    ds = (p.astype(F32) * (dp - rs_v[pl.ds(h, 1), :])).astype(BF16)
-                    dscores[h, rows(j), :] = ds
-                    dk = dk + dot_nn(ds, q)
-                    dv = dv + dot_nn(p, do)
-                return dk, dv
-
-            zero = jnp.zeros((tokens, HEAD_SIZE), F32)
-            dk, dv = lax.fori_loop(0, heads // 2, backward, (zero, zero))
-            dk = dk * scale
-            if j == 3:
-                own_kv[0] = dk
-                own_kv[1] = dv
-            elif j == 1:
-                relay_copy(2).wait_recv()
-                kv_send[1, 0] = (dk + relay[0].astype(F32)).astype(BF16)
-                kv_send[1, 1] = (dv + relay[1].astype(F32)).astype(BF16)
-                back_copy().start()
-            else:
-                kv_send[j, 0] = dk.astype(BF16)
-                kv_send[j, 1] = dv.astype(BF16)
-                if j == 0 or not odd:
-                    relay_copy(j).start()
-                else:
-                    home_copy().start()
+        kv_send[slot, 1] = value_grad(slot).astype(BF16)
+        relay_copy(slot, 1).start()
+        kv_send[slot, 0] = key_grad(slot).astype(BF16)
+        relay_copy(slot, 0).start()
+
+    def sent_back(c, grad):
+        relay_copy(0, c).wait_recv()
+        kv_send[1, c] = (grad + relay[c].astype(F32)).astype(BF16)
+        back_copy(c).start()
 
     def split(fn):
         @pl.when(core == 1)
@@ -297,7 +285,7 @@
     head_start(down_send, down_recv, down_ss, down_rs)
     hear(1)
     tell(2)
-    for i in range(4, 9):
+    for i in range(4, 10):
         loads[i].wait()
     split(pass_values_on)
 
@@ -310,10 +298,24 @@
 
     pending.append(lambda: split(window_sent))
     split(attention)
+    split(relayed)
+    sent_back(1, value_grad(1))
+    sent_back(0, key_grad(1))
+
+    @pl.when(core == 1)
+    def _():
+        give(1).wait_recv()
+        kv_send[2, 0] = key_grad(2).astype(BF16)
+        kv_send[2, 1] = value_grad(2).astype(BF16)
+        home_copy().start()
+
+    own_kv[0] = key_grad(3)
+    own_kv[1] = value_grad(3)
 
     def grads_sent(odd):
-        relay_copy(0 if odd else 2).wait_send()
-        back_copy().wait_send()
+        for c in range(2):
+            relay_copy(0 if odd else 2, c).wait_send()
+            back_copy(c).wait_send()
         if odd:
             home_copy().wait_send()
 
@@ -328,24 +330,20 @@
     def query_grads(odd):
         first = 0 if odd else tokens
         per_half = heads // 2
-
-        def one(i, acc):
-            for k in range(2):
-                h = i * 2 + k
-                dq = (dot_nn(k_t[:, first:], dscores[h, first:, :]) * scale).astype(BF16)
-                cols = pl.ds(pl.multiple_of((h % per_half) * HEAD_SIZE, HEAD_SIZE), HEAD_SIZE)
-                g_full[h // per_half, :RANK, cols] = dot_nt(down_low[:RANK, :], dq)
-                acc = acc + dot_nn(head_cols(wq_v, h), dq)
-            return acc
-
-        acc = lax.fori_loop(0, heads // 2, one, jnp.zeros((RANK, tokens), F32))
+        acc = jnp.zeros((RANK, tokens), F32)
+        for h in range(heads):
+            dq = (dot_nn(k_t[:, first:], dscores[h, first:, :]) * scale).astype(BF16)
+            col = (h % per_half) * HEAD_SIZE
+            g_full[h // per_half, :RANK, col : col + HEAD_SIZE] = dot_nt(down_low[:RANK, :], dq)
+            acc = acc + dot_nn(head_cols(wq_v, h), dq)
         upq_send[...] = acc.astype(BF16)
 
     split(query_grads)
     head_start(upq_send, upq_recv, upq_ss, upq_rs)
     hear(2)
 
-    back_copy().wait_recv()
+    for c in range(2):
+        back_copy(c).wait_recv()
 
     @pl.when(core == 0)
     def _():
@@ -354,6 +352,14 @@
 
     dkv = (own_kv[...] + kv_recv[0].astype(F32)).astype(BF16)
     kv_out[...] = dkv
+    placed = [
+        pltpu.make_async_copy(src, dst, out_sem.at[i])
+        for i, (src, dst) in enumerate([
+            (kv_out, kv_hbm), (x_out, xo_hbm), (g_out, g_hbm), (c_out, c_hbm),
+        ])
+    ]
+    placed[0].start()
+    pending.append(placed[0].wait)
     for c in range(2):
         upkv_send[c * RANK : (c + 1) * RANK, :] = dot_nt(
             wkv_v[c * RANK : (c + 1) * RANK, :], dkv[c]
@@ -466,6 +472,8 @@
             up_out[...], wd_v[:, cols], (((0,), (0,)), ((), ())), preferred_element_type=F32
         )
         x_out[:, cols] = (ADAPTER_SCALE * part).astype(BF16)
+    placed[1].start()
+    pending.append(placed[1].wait)
 
     def unit_ref(p, u):
         return g_out.at[
@@ -580,10 +588,15 @@
     for wait in pending:
         wait()
     final_copy_c(1 - core).wait_recv()
+    placed[3].start()
+    for p in range(2):
+        final_copy(p, 1 - core).wait_recv()
+    placed[2].start()
     final_copy_c(core).wait_send()
     for p in range(2):
-        final_copy(p, 1 - core).wait_recv()
         final_copy(p, core).wait_send()
+    placed[3].wait()
+    placed[2].wait()
 
 
 def place(
@@ -626,7 +639,6 @@
     vmem = pltpu.VMEM
     sem = pltpu.SemaphoreType.DMA
     anywhere = pl.BlockSpec(memory_space=pltpu.HBM)
-    in_vmem = pl.BlockSpec(memory_space=pltpu.VMEM)
     parts = pl.pallas_call(
         functools.partial(kernel, seq_count, head_count),
         out_shape=(
@@ -635,9 +647,13 @@
             jax.ShapeDtypeStruct((4 * RANK, width), F32),
             jax.ShapeDtypeStruct((2 * RANK, HEAD_SIZE), F32),
         ),
-        in_specs=[anywhere] * 5 + [pl.BlockSpec(memory_space=pltpu.SMEM)] + [anywhere] * 4,
-        out_specs=(in_vmem,) * 4,
+        in_specs=[anywhere] * 10,
+        out_specs=(anywhere,) * 4,
         scratch_shapes=[
+            vmem((2, tokens, HEAD_SIZE), BF16),
+            vmem((tokens, width), BF16),
+            vmem((4 * RANK, width), F32),
+            vmem((2 * RANK, HEAD_SIZE), F32),
             vmem((3 * RANK, tokens), BF16),
             vmem((tokens, columns), BF16),
             vmem((tokens, columns), BF16),
@@ -657,6 +673,7 @@
             vmem((3, 2, tokens, HEAD_SIZE), BF16),
             vmem((2, 2, tokens, HEAD_SIZE), BF16),
             vmem((2, tokens, HEAD_SIZE), BF16),
+            pltpu.SMEM((heads,), jnp.int32),
             vmem((3 * RANK, tokens), BF16),
             vmem((head_count, 3 * RANK, tokens), BF16),
             vmem((3 * RANK, tokens), BF16),
@@ -672,13 +689,13 @@
             vmem((2 * nz, per_owner, 8, 128), F32),
             vmem((RANK, HEAD_SIZE), F32),
             vmem((2 * nz, RANK, HEAD_SIZE), F32),
-            sem((9,)),
+            sem((10,)), sem((4,)),
             sem((2, 3)), sem((2, 4)),
             sem((head_count,)), sem((head_count,)),
             sem((head_count,)), sem((head_count,)),
             sem((head_count,)), sem((head_count,)),
-            sem, sem,
             sem((2,)), sem((2,)),
+            sem((3,)), sem((3,)),
             sem((3,)), sem((3,)),
             sem((2, nz)), sem((2 * nz,)),
             sem, sem((2 * nz,)),

time: 70.5 us -> 68.4 us (0.970)
  Pallas kernels: 69.7 us -> 67.6 us
    pallas_call x1, Pallas kernels: 67.7 us -> 65.6 us  [per_device(): pl.pallas_call(functools.partial(kernel, seq_count, head_count), out_shap...]
where the time goes in v4:
time: 68.4 us; the launch traced here: 68.3 us
  Pallas kernels  67.6 us (99%)
    pallas_call x1, Pallas kernels, per_device(): pl.pallas_call(functools.partial(kernel, seq_count, head_count), out_shap...  65.6 us
    pallas_call x1, Pallas kernels, per_device(): pl.pallas_call(place, out_shape=(jax.ShapeDtypeStruct((3 * RANK, width),...  2.04 us

profile of v4, /device:TPU:1, one launch (start us, length us, event | category | flops | bytes accessed | tf_op | source)
XLA Modules:
  0.0 68.3 jit_solution(14902085725302451560)
XLA Ops:
  0.6 65.6 %shard_map.137 = (bf16[2,256,128]{2,1,0:T(8,128)(2,1)}, bf16[256,1024]{1,0:T(8,128)(2,1)}, f32[64,1024]{1,0:T(8,128)}, f32[32,128]{1,0:T(8,128)}) custom-call(bf16[256,1024]{1,0:T(8,128)(2,1)} %q_hbm.1, bf16[256,128]{1,0:T(8,128)(2,1)} %k_hbm.1, bf16[256,128]{1,0:T(8,128)(2,1)} %v_hbm.1, bf16[256,1024]{1,0:T(8,128)(2,1)} %do_hbm.1, f32[8,256]{1,0:T(8,128)} %rs_hbm.1, ...), custom_call_target="tpu_custom_call" | custom-call | tf_op jit(solution)/shard_map/pallas_call | solution.py:642
  66.2 2.0 %shard_map.138 = (f32[48,1024]{1,0:T(8,128)}, f32[16,1024]{1,0:T(8,128)}, f32[32,128]{1,0:T(8,128)}, bf16[2,256,128]{2,1,0:T(8,128)(2,1)}, bf16[256,1024]{1,0:T(8,128)(2,1)}) custom-call(bf16[2,256,128]{2,1,0:T(8,128)(2,1)} %get-tuple-element.14.kv, bf16[256,1024]{1,0:T(8,128)(2,1)} %get-tuple-element.15.x, f32[64,1024]{1,0:T(8,128)} %get-tuple-element.16.g, ...), custom_call_target="tpu_custom_call" | custom-call | tf_op jit(solution)/shard_map/pallas_call | solution.py:714

commit v5 on v4

--- a/solution.py
+++ b/solution.py
@@ -12,7 +12,7 @@
 GROUP = 1024
 RANK = 16
 QUAD = 4
-UNITS = 16
+UNITS = 8
 LOG2E = 1.4426950408889634
 BIG = 1e30
 ADAPTER_SCALE = 2.0
@@ -36,10 +36,10 @@
     head_count,
     q_hbm, k_hbm, v_hbm, do_hbm, rs_hbm, flags_hbm, x_hbm, wd_hbm, wq_hbm, wkv_hbm,
     kv_hbm, xo_hbm, g_hbm, c_hbm,
-    kv_out, x_out, g_out, c_out, up_out, q_v, do_v, x_v, wd_v, wq_v, wkv_v, rs_v,
+    kv_out, x_out, g_out, c_out, g_low, c_low, up_out, q_v, do_v, x_v, wd_v, wq_v, wkv_v, rs_v,
     kwin, vwin, k_t, scores, tops, probs, dscores, own_kv, kv_send, kv_recv, relay,
     flags, down_send, down_recv, down_low, upq_send, upq_recv, upkv_send, upkv_recv,
-    g_full, g_pair, c_full, c_pair, units, slots, c_sum, c_slots,
+    g_full, g_pair, c_full, c_pair, units, slots, c_sum, c_send, c_slots,
     load_sem, out_sem, win_ss, win_rs, down_ss, down_rs, upq_ss, upq_rs, upkv_ss, upkv_rs,
     relay_ss, relay_rs, kv_ss, kv_rs, pair_ss, pair_rs, rs_ss, rs_rs, c_ss, c_rs,
     ag_ss, ag_rs, cag_ss, cag_rs, fin_ss, fin_rs, known,
@@ -47,7 +47,9 @@
     tokens = q_v.shape[0]
     heads = q_v.shape[1] // HEAD_SIZE
     nz = seq_count // QUAD
-    per_owner = UNITS // nz
+    owners = min(nz, UNITS)
+    stride = nz // owners
+    per_owner = UNITS // owners
     half = x_v.shape[1] // 2
     s = lax.axis_index("seq")
     hd = lax.axis_index("head")
@@ -395,14 +397,23 @@
                 up_out[first:last, :], x_v[:, c * half : (c + 1) * half]
             )
 
-    def far_first(i):
-        return nz // 2 + lax.rem(i + 1, 2) * (i // 2) - lax.rem(i, 2) * ((i + 1) // 2)
-
-    def scatter_copy(p, by, x):
-        slot = x * nz + by
+    def far_first(n, i):
+        return n // 2 + lax.rem(i + 1, 2) * (i // 2) - lax.rem(i, 2) * ((i + 1) // 2)
+
+    def owner_at(by):
+        return lax.rem(zi // stride + by, owners)
+
+    def scatter_copy(p, owner):
+        slot = x_lo * nz + zi
         return remote(
-            units.at[p, z_at(by)], slots.at[slot], rs_ss.at[p, by], rs_rs.at[slot], chip(by, p)
+            units.at[p, owner], slots.at[slot], rs_ss.at[p, owner], rs_rs.at[slot],
+            owner * stride * QUAD + p * 2 + core,
         )
+
+    def arrived(z, x):
+        slot = x * nz + z
+        remote(units.at[0, 0], slots.at[slot], rs_ss.at[0, 0], rs_rs.at[slot], sibling).wait_recv()
+        return slots[slot].astype(F32)
 
     def loop(first, last, fn):
         def body(i, _):
@@ -411,28 +422,25 @@
 
         lax.fori_loop(first, last, body, 0)
 
-    def at_x(p, fn):
-        @pl.when(x_lo == p)
+    def is_owner(p):
+        return jnp.logical_and(x_lo == p, lax.rem(zi, stride) == 0)
+
+    def each_owner(p, fn):
+        loop(0, owners - 1, lambda i: fn(owner_at(far_first(owners, i))))
+
+        @pl.when(jnp.logical_not(is_owner(p)))
         def _():
-            fn(nz - 1)
-
-        @pl.when(x_lo != p)
-        def _():
-            fn(nz)
+            fn(zi // stride)
 
     def scatter(p):
         pair_copy(p).wait_recv()
         at = pl.ds(p * part_rows, part_rows)
-        g = g_full[core, at, :] + g_pair[at, :]
+        g = (g_full[core, at, :] + g_pair[at, :]).astype(BF16)
         for u in range(UNITS):
-            r, col = (u // 4) * 8, (u % 4) * 128
-            units[p, u // per_owner, u % per_owner] = g[r : r + 8, col : col + 128]
-        at_x(p, lambda n: loop(0, n, lambda i: scatter_copy(p, far_first(i), x_lo).start()))
-        pending.append(
-            lambda: at_x(
-                p, lambda n: loop(0, n, lambda i: scatter_copy(p, far_first(i), x_lo).wait_send())
-            )
-        )
+            r, col = (u // 4) * 16, (u % 4) * 128
+            units[p, u // per_owner, u % per_owner] = g[r : r + 16, col : col + 128]
+        each_owner(p, lambda owner: scatter_copy(p, owner).start())
+        pending.append(lambda: each_owner(p, lambda owner: scatter_copy(p, owner).wait_send()))
 
     up_out[:RANK, :] = head_total(upq_send, upq_recv, upq_ss, upq_rs)
     down_rows(0, RANK)
@@ -440,14 +448,15 @@
     pending.append(lambda: pair_copy(0).wait_send())
     scatter(0)
 
-    c_owner = (nz // 2) * QUAD + 2 + core
+    c_owner = ((nz // 2 + 1) % nz) * QUAD + 2 + core
     is_c_owner = s == c_owner
 
     def c_copy(slot):
-        return remote(c_sum, c_slots.at[slot], c_ss, c_rs.at[slot], c_owner)
+        return remote(c_send, c_slots.at[slot], c_ss, c_rs.at[slot], c_owner)
 
     pair_copy_c().wait_recv()
     c_sum[...] = c_full[core] + c_pair[...]
+    c_send[...] = c_sum[...].astype(BF16)
 
     @pl.when(jnp.logical_not(is_c_owner))
     def _():
@@ -476,8 +485,8 @@
     pending.append(placed[1].wait)
 
     def unit_ref(p, u):
-        return g_out.at[
-            pl.ds(pl.multiple_of(p * part_rows + (u // 4) * 8, 8), 8),
+        return g_low.at[
+            pl.ds(pl.multiple_of(p * part_rows + (u // 4) * 16, 16), 16),
             pl.ds(pl.multiple_of(core * half + (u % 4) * 128, 128), 128),
         ]
 
@@ -489,42 +498,42 @@
         )
 
     def each_target(p, fn):
-        loop(0, nz - 1, lambda i: (fn(far_first(i), 0), fn(far_first(i), 1)))
+        loop(0, nz - 1, lambda i: (fn(far_first(nz, i), 0), fn(far_first(nz, i), 1)))
         fn(0, 1 - p)
 
     def gather(p):
-        @pl.when(x_lo == p)
+        @pl.when(is_owner(p))
         def _():
-            total = units[p, zi]
+            mine = zi // stride
+            total = units[p, mine].astype(F32)
             for by in range(0, nz):
                 for x in (p, 1 - p):
                     if by == 0 and x == p:
                         continue
-                    scatter_copy(p, by, x).wait_recv()
-                    total = total + slots[x * nz + by]
-            total = total * multiplier
+                    total = total + arrived(z_at(by), x)
+            total = (total * multiplier).astype(BF16)
             for i in range(per_owner):
-                unit_ref(p, zi * per_owner + i)[...] = total[i]
+                unit_ref(p, mine * per_owner + i)[...] = total[i]
 
             def start(by, x):
                 for i in range(per_owner):
-                    gather_copy(p, zi, i, by, x).start()
+                    gather_copy(p, mine, i, by, x).start()
 
             each_target(p, start)
 
     def gather_sent():
         for p in range(2):
 
-            @pl.when(x_lo == p)
+            @pl.when(is_owner(p))
             def _():
                 def wait(by, x):
                     for i in range(per_owner):
-                        gather_copy(p, zi, i, by, x).wait_send()
+                        gather_copy(p, zi // stride, i, by, x).wait_send()
 
                 each_target(p, wait)
 
     def c_ref():
-        return c_out.at[pl.ds(pl.multiple_of(core * RANK, RANK), RANK), :]
+        return c_low.at[pl.ds(pl.multiple_of(core * RANK, RANK), RANK), :]
 
     def c_gather_copy(by, x):
         return remote(c_ref(), c_ref(), cag_ss.at[x * nz + by], cag_rs, chip(by, x))
@@ -540,8 +549,8 @@
                     continue
                 slot = x * nz + z_at(by)
                 c_copy(slot).wait_recv()
-                total = total + c_slots[slot]
-        c_out[pl.ds(pl.multiple_of(core * RANK, RANK), RANK), :] = total * multiplier
+                total = total + c_slots[slot].astype(F32)
+        c_ref()[...] = (total * multiplier).astype(BF16)
         each_target(1, lambda by, x: c_gather_copy(by, x).start())
 
     def c_gather_sent():
@@ -554,24 +563,20 @@
     pending.append(c_gather_sent)
 
     def wait_gathered(p):
-        def wait(by):
+        def wait(owner):
             for i in range(per_owner):
-                gather_copy(p, z_at(by), i, by, 0).wait_recv()
-
-        loop(1, nz, wait)
-
-        @pl.when(x_lo != p)
-        def _():
-            wait(0)
+                gather_copy(p, owner, i, 0, 0).wait_recv()
+
+        each_owner(p, wait)
 
     def final_copy(p, side):
-        ref = g_out.at[
+        ref = g_low.at[
             pl.ds(p * part_rows, part_rows), pl.ds(pl.multiple_of(side * half, 128), half)
         ]
         return remote(ref, ref, fin_ss.at[p], fin_rs.at[p], sibling)
 
     def final_copy_c(side):
-        ref = c_out.at[pl.ds(pl.multiple_of(side * RANK, RANK), RANK), :]
+        ref = c_low.at[pl.ds(pl.multiple_of(side * RANK, RANK), RANK), :]
         return remote(ref, ref, fin_ss.at[2], fin_rs.at[2], sibling)
 
     wait_gathered(0)
@@ -588,9 +593,11 @@
     for wait in pending:
         wait()
     final_copy_c(1 - core).wait_recv()
+    c_out[...] = c_low[...].astype(F32)
     placed[3].start()
     for p in range(2):
         final_copy(p, 1 - core).wait_recv()
+    g_out[...] = g_low[...].astype(F32)
     placed[2].start()
     final_copy_c(core).wait_send()
     for p in range(2):
@@ -633,7 +640,8 @@
     heads = columns // HEAD_SIZE
     width = inputs.shape[1]
     nz = seq_count // QUAD
-    per_owner = UNITS // nz
+    owners = min(nz, UNITS)
+    per_owner = UNITS // owners
     flat_down = adapter_down_weight.reshape(3 * RANK, width)
     flat_kv_up = key_value_up_weight.reshape(2 * RANK, HEAD_SIZE)
     vmem = pltpu.VMEM
@@ -654,6 +662,8 @@
             vmem((tokens, width), BF16),
             vmem((4 * RANK, width), F32),
             vmem((2 * RANK, HEAD_SIZE), F32),
+            vmem((4 * RANK, width), BF16),
+            vmem((2 * RANK, HEAD_SIZE), BF16),
             vmem((3 * RANK, tokens), BF16),
             vmem((tokens, columns), BF16),
             vmem((tokens, columns), BF16),
@@ -685,10 +695,11 @@
             vmem((4 * RANK, width // 2), F32),
             vmem((2, RANK, HEAD_SIZE), F32),
             vmem((RANK, HEAD_SIZE), F32),
-            vmem((2, nz, per_owner, 8, 128), F32),
-            vmem((2 * nz, per_owner, 8, 128), F32),
+            vmem((2, owners, per_owner, 16, 128), BF16),
+            vmem((2 * nz, per_owner, 16, 128), BF16),
             vmem((RANK, HEAD_SIZE), F32),
-            vmem((2 * nz, RANK, HEAD_SIZE), F32),
+            vmem((RANK, HEAD_SIZE), BF16),
+            vmem((2 * nz, RANK, HEAD_SIZE), BF16),
             sem((10,)), sem((4,)),
             sem((2, 3)), sem((2, 4)),
             sem((head_count,)), sem((head_count,)),
@@ -697,7 +708,7 @@
             sem((2,)), sem((2,)),
             sem((3,)), sem((3,)),
             sem((3,)), sem((3,)),
-            sem((2, nz)), sem((2 * nz,)),
+            sem((2, owners)), sem((2 * nz,)),
             sem, sem((2 * nz,)),
             sem((2 * nz * per_owner,)), sem((2, UNITS)),
             sem((2 * nz,)), sem,

time: 68.4 us -> 61.6 us (0.901)
  Pallas kernels: 67.6 us -> 60.9 us
    pallas_call x1, Pallas kernels: 65.6 us -> 58.8 us  [per_device(): pl.pallas_call(functools.partial(kernel, seq_count, head_count), out_shap...]
where the time goes in v5:
time: 61.6 us; the launch traced here: 61.5 us
  Pallas kernels  60.9 us (99%)
  between operations  0.64 us (1%)
    pallas_call x1, Pallas kernels, per_device(): pl.pallas_call(functools.partial(kernel, seq_count, head_count), out_shap...  58.8 us
    pallas_call x1, Pallas kernels, per_device(): pl.pallas_call(place, out_shape=(jax.ShapeDtypeStruct((3 * RANK, width),...  2.04 us

profile of v5, /device:TPU:1, one launch (start us, length us, event | category | flops | bytes accessed | tf_op | source)
XLA Modules:
  0.0 61.5 jit_solution(7940818939060707069)
XLA Ops:
  0.6 58.8 %shard_map.137 = (bf16[2,256,128]{2,1,0:T(8,128)(2,1)}, bf16[256,1024]{1,0:T(8,128)(2,1)}, f32[64,1024]{1,0:T(8,128)}, f32[32,128]{1,0:T(8,128)}) custom-call(bf16[256,1024]{1,0:T(8,128)(2,1)} %q_hbm.1, bf16[256,128]{1,0:T(8,128)(2,1)} %k_hbm.1, bf16[256,128]{1,0:T(8,128)(2,1)} %v_hbm.1, bf16[256,1024]{1,0:T(8,128)(2,1)} %do_hbm.1, f32[8,256]{1,0:T(8,128)} %rs_hbm.1, ...), custom_call_target="tpu_custom_call" | custom-call | tf_op jit(solution)/shard_map/pallas_call | solution.py:650
  59.5 2.0 %shard_map.138 = (f32[48,1024]{1,0:T(8,128)}, f32[16,1024]{1,0:T(8,128)}, f32[32,128]{1,0:T(8,128)}, bf16[2,256,128]{2,1,0:T(8,128)(2,1)}, bf16[256,1024]{1,0:T(8,128)(2,1)}) custom-call(bf16[2,256,128]{2,1,0:T(8,128)(2,1)} %get-tuple-element.14.kv, bf16[256,1024]{1,0:T(8,128)(2,1)} %get-tuple-element.15.x, f32[64,1024]{1,0:T(8,128)} %get-tuple-element.16.g, ...), custom_call_target="tpu_custom_call" | custom-call | tf_op jit(solution)/shard_map/pallas_call | solution.py:725

commit v6 on v5

--- a/solution.py
+++ b/solution.py
@@ -12,6 +12,7 @@
 GROUP = 1024
 RANK = 16
 QUAD = 4
+ROW = 4
 UNITS = 8
 LOG2E = 1.4426950408889634
 BIG = 1e30
@@ -38,9 +39,9 @@
     kv_hbm, xo_hbm, g_hbm, c_hbm,
     kv_out, x_out, g_out, c_out, g_low, c_low, up_out, q_v, do_v, x_v, wd_v, wq_v, wkv_v, rs_v,
     kwin, vwin, k_t, scores, tops, probs, dscores, own_kv, kv_send, kv_recv, relay,
-    flags, down_send, down_recv, down_low, upq_send, upq_recv, upkv_send, upkv_recv,
+    flags, down_send, down_recv, down_low, up_send, up_recv, near_send, near_recv,
     g_full, g_pair, c_full, c_pair, units, slots, c_sum, c_send, c_slots,
-    load_sem, out_sem, win_ss, win_rs, down_ss, down_rs, upq_ss, upq_rs, upkv_ss, upkv_rs,
+    load_sem, out_sem, win_ss, win_rs, down_ss, down_rs, up_ss, up_rs, near_ss, near_rs,
     relay_ss, relay_rs, kv_ss, kv_rs, pair_ss, pair_rs, rs_ss, rs_rs, c_ss, c_rs,
     ag_ss, ag_rs, cag_ss, cag_rs, fin_ss, fin_rs, known,
 ):
@@ -67,6 +68,13 @@
     def head_at(by):
         return lax.rem(hd + by + head_count, head_count)
 
+    in_row = min(ROW, head_count)
+
+    def row_at(by):
+        return hd // in_row * in_row + lax.rem(hd % in_row + by + in_row, in_row)
+
+    other_row = lax.rem(hd + in_row, head_count)
+
     def z_at(by):
         return lax.rem(zi + by + nz, nz)
 
@@ -78,6 +86,14 @@
             src_ref=src, dst_ref=dst, send_sem=ss, recv_sem=rs,
             device_id={"seq": target}, device_id_type=MESH,
         )
+
+    barrier = pltpu.get_barrier_semaphore()
+    near = [sibling, seq_at(2), seq_at(-2), seq_at(4), seq_at(-4)]
+    for target in near:
+        pl.semaphore_signal(barrier, inc=1, device_id={"seq": target}, device_id_type=MESH)
+    near_heads = [row_at(1), row_at(-1)] + ([other_row] if head_count > ROW else [])
+    for target in near_heads:
+        pl.semaphore_signal(barrier, inc=1, device_id={"head": target}, device_id_type=MESH)
 
     loads = [
         pltpu.make_async_copy(src, dst, load_sem.at[i])
@@ -89,13 +105,7 @@
     for copy in loads:
         copy.start()
 
-    barrier = pltpu.get_barrier_semaphore()
-    near = [sibling, seq_at(2), seq_at(-2), seq_at(4), seq_at(-4)]
-    for target in near:
-        pl.semaphore_signal(barrier, inc=1, device_id={"seq": target}, device_id_type=MESH)
-    for by in range(1, head_count):
-        pl.semaphore_signal(barrier, inc=1, device_id={"head": head_at(by)}, device_id_type=MESH)
-    pl.semaphore_wait(barrier, len(near) + head_count - 1)
+    pl.semaphore_wait(barrier, len(near) + len(near_heads))
 
     rounds = []
     step = 2
@@ -114,6 +124,18 @@
         if i < len(rounds):
             pl.semaphore_wait(known.at[i], 2)
 
+    def tell_heads(i):
+        targets = [row_at(1), row_at(-1)] if i == 0 else [other_row]
+        if i == 0 or head_count > ROW:
+            for target in targets:
+                pl.semaphore_signal(
+                    known.at[3 + i], inc=1, device_id={"head": target}, device_id_type=MESH
+                )
+
+    def hear_heads(i):
+        if i == 0 or head_count > ROW:
+            pl.semaphore_wait(known.at[3 + i], 2 - i)
+
     own = (k_hbm, v_hbm)
     win = (kwin, vwin)
 
@@ -134,6 +156,7 @@
             give(c).start()
 
     tell(0)
+    tell_heads(0)
 
     def head_copy(src, dst, ss, rs, by):
         return pltpu.make_async_remote_copy(
@@ -182,6 +205,8 @@
     down_send[...] = down_part.astype(BF16)
     hear(0)
     tell(1)
+    hear_heads(0)
+    tell_heads(1)
 
     def rest_of_scores(odd):
         if odd:
@@ -212,6 +237,14 @@
         return remote(
             kv_send.at[1, c], kv_recv.at[0, c], kv_ss.at[c], kv_rs.at[c], seq_at(-2)
         )
+
+    def near_copy():
+        return remote(near_send, near_recv, near_ss, near_rs, seq_at(-2))
+
+    def projected(grads):
+        return [
+            dot_nt(wkv_v[c * RANK : (c + 1) * RANK, :], grads[c]) for c in range(2)
+        ]
 
     def home_copy():
         return remote(kv_send.at[2], kv_recv.at[1], kv_ss.at[2], kv_rs.at[2], sibling)
@@ -272,6 +305,10 @@
     def sent_back(c, grad):
         relay_copy(0, c).wait_recv()
         kv_send[1, c] = (grad + relay[c].astype(F32)).astype(BF16)
+        if c == 0:
+            for i, part in enumerate(projected(kv_send[1])):
+                near_send[i * RANK : (i + 1) * RANK, :] = part.astype(BF16)
+            near_copy().start()
         back_copy(c).start()
 
     def split(fn):
@@ -284,6 +321,7 @@
             fn(False)
 
     split(rest_of_scores)
+    hear_heads(1)
     head_start(down_send, down_recv, down_ss, down_rs)
     hear(1)
     tell(2)
@@ -318,6 +356,7 @@
         for c in range(2):
             relay_copy(0 if odd else 2, c).wait_send()
             back_copy(c).wait_send()
+        near_copy().wait_send()
         if odd:
             home_copy().wait_send()
 
@@ -338,20 +377,27 @@
             col = (h % per_half) * HEAD_SIZE
             g_full[h // per_half, :RANK, col : col + HEAD_SIZE] = dot_nt(down_low[:RANK, :], dq)
             acc = acc + dot_nn(head_cols(wq_v, h), dq)
-        upq_send[...] = acc.astype(BF16)
+        up_send[:RANK, :] = acc.astype(BF16)
 
     split(query_grads)
-    head_start(upq_send, upq_recv, upq_ss, upq_rs)
     hear(2)
-
-    for c in range(2):
-        back_copy(c).wait_recv()
 
     @pl.when(core == 0)
     def _():
         home_copy().wait_recv()
         own_kv[...] = own_kv[...] + kv_recv[1].astype(F32)
 
+    own_part = projected(own_kv[...].astype(BF16))
+    near_copy().wait_recv()
+    for c in range(2):
+        at = slice((c + 1) * RANK, (c + 2) * RANK)
+        up_send[at, :] = (
+            own_part[c] + near_recv[c * RANK : (c + 1) * RANK, :].astype(F32)
+        ).astype(BF16)
+    head_start(up_send, up_recv, up_ss, up_rs)
+
+    for c in range(2):
+        back_copy(c).wait_recv()
     dkv = (own_kv[...] + kv_recv[0].astype(F32)).astype(BF16)
     kv_out[...] = dkv
     placed = [
@@ -363,11 +409,6 @@
     placed[0].start()
     pending.append(placed[0].wait)
     for c in range(2):
-        upkv_send[c * RANK : (c + 1) * RANK, :] = dot_nt(
-            wkv_v[c * RANK : (c + 1) * RANK, :], dkv[c]
-        ).astype(BF16)
-    head_start(upkv_send, upkv_recv, upkv_ss, upkv_rs)
-    for c in range(2):
         c_full[c] = dot_nn(down_low[(c + 1) * RANK : (c + 2) * RANK, :], dkv[c])
 
     part_rows = 2 * RANK
@@ -383,19 +424,6 @@
 
     pair_copy_c().start()
     pending.append(lambda: pair_copy_c().wait_send())
-
-    def head_total(send, recv, ss, rs):
-        total = send[...].astype(F32)
-        for by in range(1, head_count):
-            head_copy(send, recv, ss, rs, by).wait_recv()
-            total = total + recv[by].astype(F32)
-        return total.astype(BF16)
-
-    def down_rows(first, last):
-        for c in range(2):
-            g_full[c, RANK + first : RANK + last, :] = dot_nn(
-                up_out[first:last, :], x_v[:, c * half : (c + 1) * half]
-            )
 
     def far_first(n, i):
         return n // 2 + lax.rem(i + 1, 2) * (i // 2) - lax.rem(i, 2) * ((i + 1) // 2)
@@ -442,12 +470,6 @@
         each_owner(p, lambda owner: scatter_copy(p, owner).start())
         pending.append(lambda: each_owner(p, lambda owner: scatter_copy(p, owner).wait_send()))
 
-    up_out[:RANK, :] = head_total(upq_send, upq_recv, upq_ss, upq_rs)
-    down_rows(0, RANK)
-    pair_copy(0).start()
-    pending.append(lambda: pair_copy(0).wait_send())
-    scatter(0)
-
     c_owner = ((nz // 2 + 1) % nz) * QUAD + 2 + core
     is_c_owner = s == c_owner
 
@@ -469,11 +491,33 @@
 
     pending.append(c_sent)
 
-    up_out[RANK:, :] = head_total(upkv_send, upkv_recv, upkv_ss, upkv_rs)
-    down_rows(RANK, 3 * RANK)
-    pair_copy(1).start()
-    pending.append(lambda: pair_copy(1).wait_send())
-    scatter(1)
+    up = up_send[...].astype(F32)
+    for by in range(1, head_count):
+        head_copy(up_send, up_recv, up_ss, up_rs, by).wait_recv()
+        up = up + up_recv[by].astype(F32)
+    up_out[...] = up.astype(BF16)
+
+    def down_rows(c):
+        g_full[c, RANK:, :] = dot_nn(up_out[...], x_v[:, c * half : (c + 1) * half])
+
+    def pair_sums(side):
+        down_rows(1 - side)
+        for p in range(2):
+            pair_copy(p).start()
+        down_rows(side)
+
+    @pl.when(core == 0)
+    def _():
+        pair_sums(0)
+
+    @pl.when(core == 1)
+    def _():
+        pair_sums(1)
+
+    for p in range(2):
+        pending.append(lambda p=p: pair_copy(p).wait_send())
+    for p in range(2):
+        scatter(p)
 
     for c in range(4):
         cols = slice(c * half // 2, (c + 1) * half // 2)
@@ -559,8 +603,8 @@
             each_target(1, lambda by, x: c_gather_copy(by, x).wait_send())
 
     gather(1)
-    pending.append(gather_sent)
-    pending.append(c_gather_sent)
+    for wait in pending:
+        wait()
 
     def wait_gathered(p):
         def wait(owner):
@@ -590,8 +634,8 @@
     wait_gathered(1)
     final_copy(1, core).start()
 
-    for wait in pending:
-        wait()
+    gather_sent()
+    c_gather_sent()
     final_copy_c(1 - core).wait_recv()
     c_out[...] = c_low[...].astype(F32)
     placed[3].start()
@@ -687,10 +731,10 @@
             vmem((3 * RANK, tokens), BF16),
             vmem((head_count, 3 * RANK, tokens), BF16),
             vmem((3 * RANK, tokens), BF16),
-            vmem((RANK, tokens), BF16),
-            vmem((head_count, RANK, tokens), BF16),
+            vmem((3 * RANK, tokens), BF16),
+            vmem((head_count, 3 * RANK, tokens), BF16),
             vmem((2 * RANK, tokens), BF16),
-            vmem((head_count, 2 * RANK, tokens), BF16),
+            vmem((2 * RANK, tokens), BF16),
             vmem((2, 4 * RANK, width // 2), F32),
             vmem((4 * RANK, width // 2), F32),
             vmem((2, RANK, HEAD_SIZE), F32),
@@ -704,7 +748,7 @@
             sem((2, 3)), sem((2, 4)),
             sem((head_count,)), sem((head_count,)),
             sem((head_count,)), sem((head_count,)),
-            sem((head_count,)), sem((head_count,)),
+            sem, sem,
             sem((2,)), sem((2,)),
             sem((3,)), sem((3,)),
             sem((3,)), sem((3,)),
@@ -713,7 +757,7 @@
             sem((2 * nz * per_owner,)), sem((2, UNITS)),
             sem((2 * nz,)), sem,
             sem((3,)), sem((3,)),
-            pltpu.SemaphoreType.REGULAR((3,)),
+            pltpu.SemaphoreType.REGULAR((5,)),
         ],
         compiler_params=pltpu.CompilerParams(
             collective_id=0, has_side_effects=True, vmem_limit_bytes=VMEM_BYTES

time: 61.6 us -> 59.1 us (0.959)
  Pallas kernels: 60.9 us -> 58.3 us
    pallas_call x1, Pallas kernels: 58.8 us -> 56.2 us  [per_device(): pl.pallas_call(functools.partial(kernel, seq_count, head_count), out_shap...]
where the time goes in v6:
time: 59.1 us; the launch traced here: 58.9 us
  Pallas kernels  58.3 us (99%)
  between operations  0.64 us (1%)
    pallas_call x1, Pallas kernels, per_device(): pl.pallas_call(functools.partial(kernel, seq_count, head_count), out_shap...  56.2 us
    pallas_call x1, Pallas kernels, per_device(): pl.pallas_call(place, out_shape=(jax.ShapeDtypeStruct((3 * RANK, width),...  2.04 us

profile of v6, /device:TPU:1, one launch (start us, length us, event | category | flops | bytes accessed | tf_op | source)
XLA Modules:
  0.0 58.9 jit_solution(16159000462540033033)
XLA Ops:
  0.6 56.2 %shard_map.137 = (bf16[2,256,128]{2,1,0:T(8,128)(2,1)}, bf16[256,1024]{1,0:T(8,128)(2,1)}, f32[64,1024]{1,0:T(8,128)}, f32[32,128]{1,0:T(8,128)}) custom-call(bf16[256,1024]{1,0:T(8,128)(2,1)} %q_hbm.1, bf16[256,128]{1,0:T(8,128)(2,1)} %k_hbm.1, bf16[256,128]{1,0:T(8,128)(2,1)} %v_hbm.1, bf16[256,1024]{1,0:T(8,128)(2,1)} %do_hbm.1, f32[8,256]{1,0:T(8,128)} %rs_hbm.1, ...), custom_call_target="tpu_custom_call" | custom-call | tf_op jit(solution)/shard_map/pallas_call | solution.py:694
  56.9 2.0 %shard_map.138 = (f32[48,1024]{1,0:T(8,128)}, f32[16,1024]{1,0:T(8,128)}, f32[32,128]{1,0:T(8,128)}, bf16[2,256,128]{2,1,0:T(8,128)(2,1)}, bf16[256,1024]{1,0:T(8,128)(2,1)}) custom-call(bf16[2,256,128]{2,1,0:T(8,128)(2,1)} %get-tuple-element.14.kv, bf16[256,1024]{1,0:T(8,128)(2,1)} %get-tuple-element.15.x, f32[64,1024]{1,0:T(8,128)} %get-tuple-element.16.g, ...), custom_call_target="tpu_custom_call" | custom-call | tf_op jit(solution)/shard_map/pallas_call | solution.py:769

commit v7 on v6

--- a/solution.py
+++ b/solution.py
@@ -13,7 +13,7 @@
 RANK = 16
 QUAD = 4
 ROW = 4
-UNITS = 8
+UNITS = 4
 LOG2E = 1.4426950408889634
 BIG = 1e30
 ADAPTER_SCALE = 2.0
@@ -435,7 +435,7 @@
         slot = x_lo * nz + zi
         return remote(
             units.at[p, owner], slots.at[slot], rs_ss.at[p, owner], rs_rs.at[slot],
-            owner * stride * QUAD + p * 2 + core,
+            (owner * stride + p * (stride // 2)) * QUAD + p * 2 + core,
         )
 
     def arrived(z, x):
@@ -451,7 +451,7 @@
         lax.fori_loop(first, last, body, 0)
 
     def is_owner(p):
-        return jnp.logical_and(x_lo == p, lax.rem(zi, stride) == 0)
+        return jnp.logical_and(x_lo == p, lax.rem(zi, stride) == p * (stride // 2))
 
     def each_owner(p, fn):
         loop(0, owners - 1, lambda i: fn(owner_at(far_first(owners, i))))
@@ -465,8 +465,7 @@
         at = pl.ds(p * part_rows, part_rows)
         g = (g_full[core, at, :] + g_pair[at, :]).astype(BF16)
         for u in range(UNITS):
-            r, col = (u // 4) * 16, (u % 4) * 128
-            units[p, u // per_owner, u % per_owner] = g[r : r + 16, col : col + 128]
+            units[p, u // per_owner, u % per_owner] = g[:, u * 128 : (u + 1) * 128]
         each_owner(p, lambda owner: scatter_copy(p, owner).start())
         pending.append(lambda: each_owner(p, lambda owner: scatter_copy(p, owner).wait_send()))
 
@@ -530,8 +529,8 @@
 
     def unit_ref(p, u):
         return g_low.at[
-            pl.ds(pl.multiple_of(p * part_rows + (u // 4) * 16, 16), 16),
-            pl.ds(pl.multiple_of(core * half + (u % 4) * 128, 128), 128),
+            pl.ds(p * part_rows, part_rows),
+            pl.ds(pl.multiple_of(core * half + u * 128, 128), 128),
         ]
 
     def gather_copy(p, owner, i, by, x):
@@ -739,8 +738,8 @@
             vmem((4 * RANK, width // 2), F32),
             vmem((2, RANK, HEAD_SIZE), F32),
             vmem((RANK, HEAD_SIZE), F32),
-            vmem((2, owners, per_owner, 16, 128), BF16),
-            vmem((2 * nz, per_owner, 16, 128), BF16),
+            vmem((2, owners, per_owner, 2 * RANK, 128), BF16),
+            vmem((2 * nz, per_owner, 2 * RANK, 128), BF16),
             vmem((RANK, HEAD_SIZE), F32),
             vmem((RANK, HEAD_SIZE), BF16),
             vmem((2 * nz, RANK, HEAD_SIZE), BF16),

time: 59.1 us -> 56.5 us (0.956)
  Pallas kernels: 58.3 us -> 55.7 us
    pallas_call x1, Pallas kernels: 56.2 us -> 53.7 us  [per_device(): pl.pallas_call(functools.partial(kernel, seq_count, head_count), out_shap...]
where the time goes in v7:
time: 56.5 us; the launch traced here: 56.4 us
  Pallas kernels  55.7 us (99%)
  between operations  0.64 us (1%)
    pallas_call x1, Pallas kernels, per_device(): pl.pallas_call(functools.partial(kernel, seq_count, head_count), out_shap...  53.7 us
    pallas_call x1, Pallas kernels, per_device(): pl.pallas_call(place, out_shape=(jax.ShapeDtypeStruct((3 * RANK, width),...  2.04 us

profile of v7, /device:TPU:1, one launch (start us, length us, event | category | flops | bytes accessed | tf_op | source)
XLA Modules:
  0.0 56.4 jit_solution(6849962384477440253)
XLA Ops:
  0.6 53.7 %shard_map.137 = (bf16[2,256,128]{2,1,0:T(8,128)(2,1)}, bf16[256,1024]{1,0:T(8,128)(2,1)}, f32[64,1024]{1,0:T(8,128)}, f32[32,128]{1,0:T(8,128)}) custom-call(bf16[256,1024]{1,0:T(8,128)(2,1)} %q_hbm.1, bf16[256,128]{1,0:T(8,128)(2,1)} %k_hbm.1, bf16[256,128]{1,0:T(8,128)(2,1)} %v_hbm.1, bf16[256,1024]{1,0:T(8,128)(2,1)} %do_hbm.1, f32[8,256]{1,0:T(8,128)} %rs_hbm.1, ...), custom_call_target="tpu_custom_call" | custom-call | tf_op jit(solution)/shard_map/pallas_call | solution.py:693
  54.3 2.0 %shard_map.138 = (f32[48,1024]{1,0:T(8,128)}, f32[16,1024]{1,0:T(8,128)}, f32[32,128]{1,0:T(8,128)}, bf16[2,256,128]{2,1,0:T(8,128)(2,1)}, bf16[256,1024]{1,0:T(8,128)(2,1)}) custom-call(bf16[2,256,128]{2,1,0:T(8,128)(2,1)} %get-tuple-element.14.kv, bf16[256,1024]{1,0:T(8,128)(2,1)} %get-tuple-element.15.x, f32[64,1024]{1,0:T(8,128)} %get-tuple-element.16.g, ...), custom_call_target="tpu_custom_call" | custom-call | tf_op jit(solution)/shard_map/pallas_call | solution.py:768

commit v8 on v7

--- a/solution.py
+++ b/solution.py
@@ -37,7 +37,7 @@
     head_count,
     q_hbm, k_hbm, v_hbm, do_hbm, rs_hbm, flags_hbm, x_hbm, wd_hbm, wq_hbm, wkv_hbm,
     kv_hbm, xo_hbm, g_hbm, c_hbm,
-    kv_out, x_out, g_out, c_out, g_low, c_low, up_out, q_v, do_v, x_v, wd_v, wq_v, wkv_v, rs_v,
+    kv_out, x_out, g_low, c_low, up_out, q_v, do_v, x_v, wd_v, wq_v, wkv_v, rs_v,
     kwin, vwin, k_t, scores, tops, probs, dscores, own_kv, kv_send, kv_recv, relay,
     flags, down_send, down_recv, down_low, up_send, up_recv, near_send, near_recv,
     g_full, g_pair, c_full, c_pair, units, slots, c_sum, c_send, c_slots,
@@ -403,7 +403,7 @@
     placed = [
         pltpu.make_async_copy(src, dst, out_sem.at[i])
         for i, (src, dst) in enumerate([
-            (kv_out, kv_hbm), (x_out, xo_hbm), (g_out, g_hbm), (c_out, c_hbm),
+            (kv_out, kv_hbm), (x_out, xo_hbm), (g_low, g_hbm), (c_low, c_hbm),
         ])
     ]
     placed[0].start()
@@ -636,11 +636,9 @@
     gather_sent()
     c_gather_sent()
     final_copy_c(1 - core).wait_recv()
-    c_out[...] = c_low[...].astype(F32)
     placed[3].start()
     for p in range(2):
         final_copy(p, 1 - core).wait_recv()
-    g_out[...] = g_low[...].astype(F32)
     placed[2].start()
     final_copy_c(core).wait_send()
     for p in range(2):
@@ -650,13 +648,13 @@
 
 
 def place(
-    kv, x, g, c, down_o, up_q_o, up_kv_o, kv_o, x_o, kv_v, x_v, g_v, c_v, in_sems, out_sems
+    kv, x, g, c, down_o, up_q_o, up_kv_o, kv_o, x_o, kv_v, x_v, g_v, c_v, g_w, c_w, in_sems, out_sems
 ):
     ways = [
         (x, x_v, [(x_v, x_o)]),
-        (g, g_v, [(g_v.at[RANK:], down_o), (g_v.at[:RANK], up_q_o)]),
+        (g, g_v, [(g_w.at[RANK:], down_o), (g_w.at[:RANK], up_q_o)]),
         (kv, kv_v, [(kv_v, kv_o)]),
-        (c, c_v, [(c_v, up_kv_o)]),
+        (c, c_v, [(c_w, up_kv_o)]),
     ]
     arriving = [
         pltpu.make_async_copy(src, dst, in_sems.at[i]) for i, (src, dst, _) in enumerate(ways)
@@ -664,8 +662,11 @@
     for copy in arriving:
         copy.start()
     leaving = []
-    for copy, (_, _, targets) in zip(arriving, ways):
+    wide = {1: (g_v, g_w), 3: (c_v, c_w)}
+    for i, (copy, (_, _, targets)) in enumerate(zip(arriving, ways)):
         copy.wait()
+        if i in wide:
+            wide[i][1][...] = wide[i][0][...].astype(F32)
         for src, dst in targets:
             leaving.append(pltpu.make_async_copy(src, dst, out_sems.at[len(leaving)]))
             leaving[-1].start()
@@ -695,16 +696,14 @@
         out_shape=(
             jax.ShapeDtypeStruct((2, tokens, HEAD_SIZE), BF16),
             jax.ShapeDtypeStruct((tokens, width), BF16),
-            jax.ShapeDtypeStruct((4 * RANK, width), F32),
-            jax.ShapeDtypeStruct((2 * RANK, HEAD_SIZE), F32),
+            jax.ShapeDtypeStruct((4 * RANK, width), BF16),
+            jax.ShapeDtypeStruct((2 * RANK, HEAD_SIZE), BF16),
         ),
         in_specs=[anywhere] * 10,
         out_specs=(anywhere,) * 4,
         scratch_shapes=[
             vmem((2, tokens, HEAD_SIZE), BF16),
             vmem((tokens, width), BF16),
-            vmem((4 * RANK, width), F32),
-            vmem((2 * RANK, HEAD_SIZE), F32),
             vmem((4 * RANK, width), BF16),
             vmem((2 * RANK, HEAD_SIZE), BF16),
             vmem((3 * RANK, tokens), BF16),
@@ -779,6 +778,8 @@
         scratch_shapes=[
             vmem((2, tokens, HEAD_SIZE), BF16),
             vmem((tokens, width), BF16),
+            vmem((4 * RANK, width), BF16),
+            vmem((2 * RANK, HEAD_SIZE), BF16),
             vmem((4 * RANK, width), F32),
             vmem((2 * RANK, HEAD_SIZE), F32),
             sem((4,)),

time: 56.5 us -> 56.4 us (level)
  no operation moved by 1% of the time
where the time goes in v8:
time: 56.4 us; the launch traced here: 56.3 us
  Pallas kernels  55.6 us (99%)
  between operations  0.64 us (1%)
    pallas_call x1, Pallas kernels, per_device(): pl.pallas_call(functools.partial(kernel, seq_count, head_count), out_shap...  53.6 us
    pallas_call x1, Pallas kernels, per_device(): pl.pallas_call(place, out_shape=(jax.ShapeDtypeStruct((3 * RANK, width),...  2.04 us

profile of v8, /device:TPU:1, one launch (start us, length us, event | category | flops | bytes accessed | tf_op | source)
XLA Modules:
  0.0 56.3 jit_solution(5869364606060167948)
XLA Ops:
  0.6 53.6 %shard_map.137 = (bf16[2,256,128]{2,1,0:T(8,128)(2,1)}, bf16[256,1024]{1,0:T(8,128)(2,1)}, bf16[64,1024]{1,0:T(8,128)(2,1)}, bf16[32,128]{1,0:T(8,128)(2,1)}) custom-call(bf16[256,1024]{1,0:T(8,128)(2,1)} %q_hbm.1, bf16[256,128]{1,0:T(8,128)(2,1)} %k_hbm.1, bf16[256,128]{1,0:T(8,128)(2,1)} %v_hbm.1, bf16[256,1024]{1,0:T(8,128)(2,1)} %do_hbm.1, ...), custom_call_target="tpu_custom_call" | custom-call | tf_op jit(solution)/shard_map/pallas_call | solution.py:694
  54.3 2.0 %shard_map.138 = (f32[48,1024]{1,0:T(8,128)}, f32[16,1024]{1,0:T(8,128)}, f32[32,128]{1,0:T(8,128)}, bf16[2,256,128]{2,1,0:T(8,128)(2,1)}, bf16[256,1024]{1,0:T(8,128)(2,1)}) custom-call(bf16[2,256,128]{2,1,0:T(8,128)(2,1)} %get-tuple-element.14.kv, bf16[256,1024]{1,0:T(8,128)(2,1)} %get-tuple-element.15.x, bf16[64,1024]{1,0:T(8,128)(2,1)} %get-tuple-element.16.g, ...), custom_call_target="tpu_custom_call" | custom-call | tf_op jit(solution)/shard_map/pallas_call | solution.py:767
